TPU v7x, 32 devices: a whole 2x2x4 slice. The times are simulated.
32 devices in a mesh: groups: 2 (over y), store: 4 (over x, core), tensor: 4 (over z).
Axes of the slice: x: 2, y: 2, z: 4, core: 2. Of those that a mesh axis runs over, the one named last changes fastest.
Arguments:
- tokens: bfloat16 [2048, 8192], P(('groups', 'store'), 'tensor'), parts along dimension 0, may hold values from -6 to 6
- key_value_weight: bfloat16 [8192, 2048], P('tensor'), may hold values from -0.0625 to 0.0625
- adapter_down_maps: bfloat16 [128, 8192, 128], P(('groups', 'store'), 'tensor'), parts along dimension 0, may hold values from -0.0625 to 0.0625
- adapter_up_maps: bfloat16 [128, 64, 2048], P(('groups', 'store'), 'tensor'), parts along dimension 0, may hold values from -0.75 to 0.75
- local_adapter_ids: int32 [2048], P(('groups', 'store')), parts along dimension 0, may hold values from 0 to 15, as said below
- request_slot_index: int32 [2048], P(('groups', 'store')), parts along dimension 0, may hold values from 0 to 7, as said below
Outputs:
- kv_new: bfloat16 [2048, 2048], P(('groups', 'store'), 'tensor'), parts along dimension 0
There are 2 independent parts, one for each index of `groups`. A program takes and returns all parts, laid end to end along the dimension named above; an argument that names none is the same for every part. Nothing has to cross between parts.
Inputs may be any that keep to these rules, and one draw needn't show every extreme that they name: `local_adapter_ids`: on one device (a block of 256 requests), requests with the same slot have the same local id, and different slots of the same owner hold different local ids. request_slot_index // 2 is the index of store that owns the request's adapter. Among the 256 requests of one device at most 64 have the same owner, and on every device exactly 64 requests have one owner, whose 2 slots are all used.
All inputs are finite; a program needn't handle non-finite values.
Results may differ from a plain program's by a relative error of at most 0.0039.
Values may be sent and summed in bfloat16 or wider, within the bound.
No kernel may reach another device: no remote copies, remote signals or barrier semaphores. Data moves between devices by JAX's collectives and lax.ppermute only.
A program may use at most 128 MiB of HBM per device.

v0:
```python
import jax
import jax.numpy as jnp
from jax import lax
from jax.sharding import PartitionSpec as P

SLOTS = 2


def shards(
    tokens,
    key_value_weight,
    adapter_down_maps,
    adapter_up_maps,
    local_adapter_ids,
    request_slot_index,
):
    store_count = lax.axis_size("store")
    row_count = tokens.shape[0]
    slot_count = store_count * SLOTS
    rank_portion = adapter_up_maps.shape[1]
    half_rank = adapter_down_maps.shape[2] // 2
    width_kv = key_value_weight.shape[1] // 2
    slot_index = jnp.arange(slot_count, dtype=jnp.int32)
    chosen = request_slot_index[:, None] == slot_index[None, :]
    wanted = jnp.max(jnp.where(chosen, local_adapter_ids[:, None], 0), axis=0).reshape(
        store_count, SLOTS
    )
    requested_ids = lax.all_to_all(wanted, "store", split_axis=0, concat_axis=0, tiled=True)
    down_row_block = jnp.take(adapter_down_maps, requested_ids, axis=0)
    up_row_block = jnp.take(adapter_up_maps, requested_ids, axis=0)
    down_recv = lax.all_to_all(down_row_block, "store", split_axis=0, concat_axis=0, tiled=True)
    up_recv = lax.all_to_all(up_row_block, "store", split_axis=0, concat_axis=0, tiled=True)
    down_recv = down_recv.reshape(slot_count, down_recv.shape[2], down_recv.shape[3])
    every_slot = jnp.einsum("rd,kdc->rkc", tokens, down_recv, preferred_element_type=jnp.float32)
    low_part = jnp.einsum("rk,rkc->rc", chosen.astype(jnp.float32), every_slot)
    low_rank = lax.psum(low_part, "tensor").astype(jnp.bfloat16)
    up_recv = up_recv.reshape(slot_count, rank_portion, 2 * width_kv)
    rank_start = lax.axis_index("tensor") * rank_portion
    key_low = lax.dynamic_slice_in_dim(low_rank, rank_start, rank_portion, 1)
    value_low = lax.dynamic_slice_in_dim(low_rank, half_rank + rank_start, rank_portion, 1)
    slot_mask = chosen.astype(jnp.bfloat16)
    key_mixed = (slot_mask[:, :, None] * key_low[:, None, :]).reshape(
        row_count, slot_count * rank_portion
    )
    value_mixed = (slot_mask[:, :, None] * value_low[:, None, :]).reshape(
        row_count, slot_count * rank_portion
    )
    key_up = up_recv[:, :, :width_kv].reshape(slot_count * rank_portion, width_kv)
    value_up = up_recv[:, :, width_kv:].reshape(slot_count * rank_portion, width_kv)
    adapted = jnp.concatenate(
        [
            jnp.dot(key_mixed, key_up, preferred_element_type=jnp.float32),
            jnp.dot(value_mixed, value_up, preferred_element_type=jnp.float32),
        ],
        axis=1,
    )
    partials = jnp.dot(tokens, key_value_weight, preferred_element_type=jnp.float32) + adapted
    return lax.psum_scatter(partials, "tensor", scatter_dimension=1, tiled=True).astype(
        jnp.bfloat16
    )


def solution(mesh):
    in_specs = (
        P(("groups", "store"), "tensor"),
        P("tensor", None),
        P(("groups", "store"), "tensor", None),
        P(("groups", "store"), "tensor", None),
        P(("groups", "store")),
        P(("groups", "store")),
    )
    out_specs = P(("groups", "store"), "tensor")
    return jax.shard_map(shards, mesh=mesh, in_specs=in_specs, out_specs=out_specs, check_vma=False)
```

profile of v0, /device:TPU:0, one launch (start us, length us, event | category | flops | bytes accessed | tf_op | source)
XLA Modules:
  0.0 173.8 jit_solution(9070268435450482407)
XLA Ops:
  6.5 0.0 copy-start
  6.5 0.9 select_reduce_fusion
  7.4 0.1 all_to_all.16
  7.5 7.8 %all_to_all.25 = s32[4,1,2]{2,1,0:T(1,128)S(1)} all-to-all(s32[4,1,2]{2,1,0:T(1,128)S(1)} %bitcast.31), channel_id=1, replica_groups=mesh['groups'=2,'store'=4,'tensor'=4] {'store'}, dimensions={0} | all-to-all | bytes 64 | tf_op jit(solution)/shard_map/all_to_all | solution.py:28
  15.3 0.1 copy.18
  15.4 0.1 copy.21
  15.5 0.1 reshape.77
  15.6 6.4 %gather_fusion = bf16[8,2048,128]{2,1,0:T(8,128)(2,1)} fusion(bf16[16,2048,128]{2,1,0:T(8,128)(2,1)} %param.8, s32[1024]{0:T(1024)S(1)} %pad_clamp_fusion), kind=kCustom, calls=%fused_computation | custom fusion | bytes 8388640 | tf_op jit(solution)/shard_map/jit(_take)/gather | solution.py:29
  22.0 6.2 %copy.22 = bf16[4,2,2048,128]{2,3,1,0:T(8,128)(2,1)} copy(bf16[4,2,2048,128]{3,2,1,0:T(8,128)(2,1)} %bitcast.27) | data formatting | bytes 8388608 | tf_op jit(solution)/shard_map/jit(_take)/gather | solution.py:29
  28.2 0.1 copy.19
  28.3 4.6 %broadcast_select_fusion = bf16[4,2,2048,128]{2,3,1,0:T(8,128)(2,1)} fusion(bf16[4,2,2048,128]{2,3,1,0:T(8,128)(2,1)} %copy.22, pred[4,2]{1,0:T(4,128)(4,1)S(1)} %copy.19), kind=kLoop, calls=%fused_computation.2 | loop fusion | flops 2097152 | bytes 8388616 | tf_op jit(solution)/shard_map/jit(_take)/select_n | solution.py:29
  32.9 0.0 copy-start.2
  32.9 0.0 copy-start.1
  33.0 5.0 %all-to-all-start.1 = ((bf16[4,2,2048,128]{2,3,1,0:T(8,128)(2,1)}), bf16[4,2,2048,128]{2,3,1,0:T(8,128)(2,1)}, u32[]{:S(2)}, u32[]{:S(2)}) async-start(bf16[4,2,2048,128]{2,3,1,0:T(8,128)(2,1)} %broadcast_select_fusion), calls=%async_computation.1 | async-start | bytes 8388608 | tf_op jit(solution)/shard_map/all_to_all | solution.py:31
  38.0 0.0 copy-done.2
  38.0 0.0 copy-done.1
  38.0 0.6 gather_fusion.1
  38.6 1.0 broadcast_select_fusion.1
  39.5 46.6 %all-to-all-done.1 = bf16[4,2,2048,128]{2,3,1,0:T(8,128)(2,1)} async-done(((bf16[4,2,2048,128]{2,3,1,0:T(8,128)(2,1)}), bf16[4,2,2048,128]{2,3,1,0:T(8,128)(2,1)}, u32[]{:S(2)}, u32[]{:S(2)}) %all-to-all-start.1) | async-done | bytes 4194336 | tf_op jit(solution)/shard_map/all_to_all | solution.py:31
  86.2 3.5 %all-to-all-start.2 = ((bf16[4,2,16,2048]{3,2,1,0:T(8,128)(2,1)}), bf16[4,2,16,2048]{3,2,1,0:T(8,128)(2,1)S(1)}, u32[]{:S(2)}, u32[]{:S(2)}) async-start(bf16[4,2,16,2048]{3,2,1,0:T(8,128)(2,1)} %broadcast_select_fusion.1), calls=%async_computation.2 | async-start | bytes 1048576 | tf_op jit(solution)/shard_map/all_to_all | solution.py:32
  89.7 0.0 reduce-scatter.2.cloned.1.call-start
  89.7 0.0 copy-done
  89.7 3.5 %fusion.1 = f32[256,128]{0,1:T(8,128)S(1)} fusion(bf16[8,2048,128]{1,2,0:T(8,128)(2,1)} %bitcast.4, bf16[256,2048]{1,0:T(8,128)(2,1)S(1)} %copy-done, f32[256,8]{0,1:T(8,128)S(1)} %get-tuple-element.8), kind=kOutput, calls=%fused_computation.8 | convolution fusion | flops 1074233344 | bytes 5382144 | tf_op jit(solution)/shard_map/rd,kdc->rkc/dot_general | solution.py:34
  93.2 21.6 %all-reduce.1 = bf16[256,128]{0,1:T(8,128)(2,1)S(1)} all-reduce(f32[256,128]{0,1:T(8,128)S(1)} %fusion.1), channel_id=1, replica_groups=mesh['groups'=2,'store'=4,'tensor'=4] {'tensor'}, use_global_device_ids=true, to_apply=%region_1.2 | all-reduce | flops 32768 | bytes 196608 | tf_op jit(solution)/shard_map/psum | solution.py:36
  114.8 0.0 all-to-all-done.2
  114.9 0.3 convolution_bitcast_fusion.1
  115.2 0.3 convolution_bitcast_fusion
  115.5 7.1 %convolution_add_fusion = f32[256,2048]{1,0:T(8,128)} fusion(bf16[256,2048]{1,0:T(8,128)(2,1)S(1)} %copy-done, bf16[2048,2048]{1,0:T(8,128)(2,1)} %param.7, f32[256,1024]{1,0:T(8,128)S(1)} %convolution_bitcast_fusion, f32[256,1024]{1,0:T(8,128)S(1)} %convolution_bitcast_fusion.1), kind=kOutput, calls=%fused_computation.3 | convolution fusion | flops 2148532224 | bytes 13631488 | tf_op jit(solution)/shard_map/dot_general | solution.py:57
  122.6 0.0 reduce-scatter.2.cloned.1.call-update
  122.6 42.5 %reduce-scatter.2.cloned.1.call-done = f32[256,512]{1,0:T(8,128)} async-done(((f32[256,2048]{1,0:T(8,128)}), f32[256,512]{1,0:T(8,128)}) %reduce-scatter.2.cloned.1.call-update) | async-done | bytes 524304 | tf_op jit(solution)/shard_map/reduce_scatter | solution.py:58
  165.1 1.8 %convert_element_type.16 = bf16[256,512]{1,0:T(8,128)(2,1)} convert(f32[256,512]{1,0:T(8,128)} %reduce-scatter.2.cloned.1.call-done) | non-fusion elementwise | flops 131072 | bytes 786432 | tf_op jit(solution)/shard_map/convert_element_type | solution.py:58
  (5 shorter events, 0.0 us)
Async XLA Ops:
  6.5 83.2 %copy-start = (bf16[256,2048]{1,0:T(8,128)(2,1)S(1)}, bf16[256,2048]{1,0:T(8,128)(2,1)}, u32[]{:S(2)}) copy-start(bf16[256,2048]{1,0:T(8,128)(2,1)} %param.6) | copy-start | bytes 3145732
  32.9 5.0 %copy-start.2 = (s32[256]{0:T(256)S(1)}, s32[256]{0:T(256)}, u32[]{:S(2)}) copy-start(s32[256]{0:T(256)} %param.11) | copy-start | bytes 3076
  32.9 5.0 %copy-start.1 = (bf16[16,16,2048]{2,1,0:T(8,128)(2,1)S(1)}, bf16[16,16,2048]{2,1,0:T(8,128)(2,1)}, u32[]{:S(2)}) copy-start(bf16[16,16,2048]{2,1,0:T(8,128)(2,1)} %param.9) | copy-start | bytes 3145732
  33.0 53.2 %all-to-all-start.1 = ((bf16[4,2,2048,128]{2,3,1,0:T(8,128)(2,1)}), bf16[4,2,2048,128]{2,3,1,0:T(8,128)(2,1)}, u32[]{:S(2)}, u32[]{:S(2)}) async-start(bf16[4,2,2048,128]{2,3,1,0:T(8,128)(2,1)} %broadcast_select_fusion), calls=%async_computation.1 | async-start | bytes 8388608 | tf_op jit(solution)/shard_map/all_to_all | solution.py:31
  86.2 28.7 %all-to-all-start.2 = ((bf16[4,2,16,2048]{3,2,1,0:T(8,128)(2,1)}), bf16[4,2,16,2048]{3,2,1,0:T(8,128)(2,1)S(1)}, u32[]{:S(2)}, u32[]{:S(2)}) async-start(bf16[4,2,16,2048]{3,2,1,0:T(8,128)(2,1)} %broadcast_select_fusion.1), calls=%async_computation.2 | async-start | bytes 1048576 | tf_op jit(solution)/shard_map/all_to_all | solution.py:32
  89.7 75.5 %reduce-scatter.2.cloned.1.call-start = ((), (), s32[]{:S(2)}) async-start(), calls=%async_computation.4 | async-start | bytes 2621440 | tf_op jit(solution)/shard_map/reduce_scatter | solution.py:58
Sparse Core Ops, SparseCore 0:
  122.7 42.3 reduce-scatter.1
where the time goes:
time: 174 us
  waiting for transfers between devices  89.2 us (51%)
  blocking collectives  29.4 us (17%)
  local copies, waits for them, and re-layouts  13.7 us (8%)
  between operations  13.5 us (8%)
  matrix products  11.2 us (6%)
  starting transfers between devices  8.5 us (5%)
  other arithmetic  8.28 us (5%)
    all_to_all x1, waiting for transfers between devices, shards(): lax.all_to_all(down_row_block, 'store', split_axis=0, concat_axis=0, tile...  46.6 us
    reduce_scatter x1, waiting for transfers between devices, shards(): lax.psum_scatter(partials, 'tensor', scatter_dimension=1, tiled=True)  42.5 us
    psum x1, blocking collectives, shards(): low_rank = lax.psum(low_part, 'tensor').astype(jnp.bfloat16)  21.6 us
    gather x2, local copies, waits for them, and re-layouts, shards(): down_row_block = jnp.take(adapter_down_maps, requested_ids, axis=0)  12.7 us
    all_to_all x1, blocking collectives, shards(): lax.all_to_all(wanted, 'store', split_axis=0, concat_axis=0, tiled=True)  7.75 us
    dot_general x1, matrix products, shards(): jnp.dot(tokens, key_value_weight, preferred_element_type=jnp.float32)  7.09 us
    all_to_all x1, starting transfers between devices, shards(): lax.all_to_all(down_row_block, 'store', split_axis=0, concat_axis=0, tile...  4.99 us
    select_n x2, other arithmetic, shards(): down_row_block = jnp.take(adapter_down_maps, requested_ids, axis=0)  4.62 us
  transfers between devices with their start and end apart: 3, of which 2 were waited for; matrix products, arithmetic and copies ran while one was open for 3% of the time, Pallas kernels for 0%

commit v1 on v0

v1 whole, which is shorter than its diff:
```python
import functools

import jax
import jax.numpy as jnp
from jax import lax
from jax.experimental import pallas as pl
from jax.experimental.pallas import tpu as pltpu
from jax.sharding import PartitionSpec as P

SLOTS = 2
GROUP_ROWS = 64
LANES = 128
F32 = jnp.float32
BF16 = jnp.bfloat16
VMEM = pl.BlockSpec(memory_space=pltpu.VMEM)
HBM = pl.BlockSpec(memory_space=pl.ANY)
PARAMS = pltpu.CompilerParams(vmem_limit_bytes=48 * 1024 * 1024)


def contract(a, b, dim_a, dim_b):
    return lax.dot_general(a, b, (((dim_a,), (dim_b,)), ((), ())), preferred_element_type=F32)


def group_kernel(store_count, ids_ref, slots_ref, tokens_ref, *outs):
    place_ref, group_refs = outs[0], outs[1:]
    me = lax.axis_index("store")
    rows, width = tokens_ref.shape
    owner = slots_ref[...] // SLOTS
    relative = owner ^ me
    padded = max(8, store_count)
    mine = lax.broadcasted_iota(jnp.int32, (padded, rows), 0) == relative
    upto = lax.broadcasted_iota(jnp.int32, (rows, rows), 0) <= lax.broadcasted_iota(jnp.int32, (rows, rows), 1)
    count = contract(mine.astype(F32).astype(BF16), upto.astype(F32).astype(BF16), 1, 0)
    rank = jnp.sum(jnp.where(mine, count, 0.0), axis=0, keepdims=True).astype(jnp.int32) - 1
    tags = jnp.broadcast_to((ids_ref[...] + 1).astype(F32), (LANES, rows)).astype(BF16)
    position = lax.broadcasted_iota(jnp.int32, (GROUP_ROWS, rows), 0)
    for k, out in enumerate(group_refs):
        place = ((relative == k) & (rank == position)).astype(F32).astype(BF16)
        place_ref[k * GROUP_ROWS : (k + 1) * GROUP_ROWS, :] = place
        out[:, :width] = contract(place, tokens_ref[...], 1, 0).astype(BF16)
        out[:, width:] = contract(place, tags, 1, 1).astype(BF16)


def down_kernel(group_count, tensor_count, *refs):
    xs, down_ref = refs[:group_count], refs[group_count]
    tags_ref, pieces = refs[group_count + 1], refs[group_count + 2 : group_count + 2 + tensor_count]
    maps, low, low_t, sems = refs[group_count + 2 + tensor_count :]
    me = lax.axis_index("tensor")
    adapters, width, ranks = down_ref.shape
    copies, tops = [], []
    for g, x in enumerate(xs):
        tag = x[:, width:].astype(F32)
        top = jnp.max(tag)
        bottom = jnp.min(jnp.where(tag > 0, tag, top))
        tops.append(top)
        for slot, chosen in enumerate((bottom, top)):
            index = jnp.clip(chosen.astype(jnp.int32) - 1, 0, adapters - 1)
            copy = pltpu.make_async_copy(
                down_ref.at[index], maps.at[g, :, slot * ranks : (slot + 1) * ranks], sems.at[g, slot]
            )
            copy.start()
            copies.append(copy)
    for g, x in enumerate(xs):
        copies[2 * g].wait()
        copies[2 * g + 1].wait()
        both = contract(x[:, :width], maps[g], 1, 0)
        low[g * GROUP_ROWS : (g + 1) * GROUP_ROWS, :ranks] = jnp.where(
            x[:, width:].astype(F32) == tops[g], both[:, ranks:], both[:, :ranks]
        )
        low[g * GROUP_ROWS : (g + 1) * GROUP_ROWS, ranks:] = x[:, width:].astype(F32)
    low_t[...] = low[:, :ranks].T
    tags_ref[...] = low[:, ranks:].T[:8]
    portion = ranks // 2 // tensor_count
    for j, piece in enumerate(pieces):
        to = me ^ j
        for half in range(2):
            value = jnp.zeros((portion, low_t.shape[1]), F32)
            for b in range(tensor_count):
                start = half * (ranks // 2) + b * portion
                value = jnp.where(to == b, low_t[start : start + portion, :], value)
            piece[half * portion : (half + 1) * portion, :] = value


def base_kernel(group_count, *refs):
    xs, weight_ref, out_ref = refs[:group_count], refs[group_count], refs[group_count + 1]
    width = weight_ref.shape[0]
    for g, x in enumerate(xs):
        out_ref[g * GROUP_ROWS : (g + 1) * GROUP_ROWS, :] = contract(x[:, :width], weight_ref[...], 1, 0)


def up_kernel(group_count, tensor_count, adapters, base_ref, tags_ref, up_ref, *refs):
    pieces, outs, mixed = refs[:tensor_count], refs[tensor_count:-1], refs[-1]
    me = lax.axis_index("tensor")
    low = pieces[0][...]
    for piece in pieces[1:]:
        low = low + piece[...]
    low = low.astype(BF16).astype(F32)
    portion = low.shape[0] // 2
    tag = tags_ref[0:1, :]
    for half in range(2):
        part = low[half * portion : (half + 1) * portion, :]
        for a in range(adapters):
            mixed[half, a * portion : (a + 1) * portion, :] = jnp.where(tag == a + 1, part, 0.0)
    block = up_ref.shape[1] // tensor_count
    for j in range(tensor_count):
        to = me ^ j
        columns = pl.ds(pl.multiple_of(to * block, block), block)
        total = base_ref[:, columns] + contract(
            mixed[to // (tensor_count // 2)].astype(BF16), up_ref[:, columns], 0, 0
        )
        for g in range(group_count):
            outs[g * tensor_count + j][...] = total[g * GROUP_ROWS : (g + 1) * GROUP_ROWS, :].astype(BF16)


def finish_kernel(counts, place_ref, *refs):
    out_ref, grouped = refs[-2], refs[-1]
    first = 0
    for k, count in enumerate(counts):
        total = refs[first][...].astype(F32)
        for ref in refs[first + 1 : first + count]:
            total = total + ref[...].astype(F32)
        first += count
        grouped[k * GROUP_ROWS : (k + 1) * GROUP_ROWS, :] = total.astype(BF16)
    out_ref[...] = contract(place_ref[...], grouped[...], 0, 0).astype(BF16)


def shards(tokens, weight, down_maps, up_maps, local_ids, slot_index):
    store_count, tensor_count = lax.axis_size("store"), lax.axis_size("tensor")
    rows, width = tokens.shape
    adapters, _, ranks = down_maps.shape
    columns = weight.shape[1]
    portion = up_maps.shape[1]
    block = columns // tensor_count
    up_flat = up_maps.reshape(adapters * portion, columns)
    shape = jax.ShapeDtypeStruct

    def swap(value, k, j):
        pairs = [
            (s * tensor_count + t, (s ^ k) * tensor_count + (t ^ j))
            for s in range(store_count)
            for t in range(tensor_count)
        ]
        return lax.ppermute(value, ("store", "tensor"), pairs)

    place, *groups = pl.pallas_call(
        functools.partial(group_kernel, store_count),
        out_shape=[shape((store_count * GROUP_ROWS, rows), BF16)]
        + [shape((GROUP_ROWS, width + LANES), BF16)] * store_count,
        in_specs=[VMEM] * 3,
        out_specs=[VMEM] * (store_count + 1),
        compiler_params=PARAMS,
        name="group_rows",
    )(local_ids.reshape(1, rows), slot_index.reshape(1, rows), tokens)

    far = range(2, store_count)
    near = range(min(2, store_count))
    arrived = {}
    for k in far:
        arrived[k] = swap(groups[k], k, 0)
    for k in near:
        arrived[k] = swap(groups[k], k, 0) if k else groups[k]

    received = {}
    for part in (near, far):
        part = list(part)
        if not part:
            continue
        count = len(part)
        part_rows = count * GROUP_ROWS
        xs = [arrived[k] for k in part]
        tags, *pieces = pl.pallas_call(
            functools.partial(down_kernel, count, tensor_count),
            out_shape=[shape((8, part_rows), F32)] + [shape((2 * portion, part_rows), F32)] * tensor_count,
            in_specs=[VMEM] * count + [HBM],
            out_specs=[VMEM] * (tensor_count + 1),
            scratch_shapes=[
                pltpu.VMEM((count, width, 2 * ranks), BF16),
                pltpu.VMEM((part_rows, 2 * ranks), F32),
                pltpu.VMEM((ranks, part_rows), F32),
                pltpu.SemaphoreType.DMA((count, 2)),
            ],
            compiler_params=PARAMS,
            cost_estimate=pl.CostEstimate(
                flops=4 * part_rows * width * ranks, bytes_accessed=count * 4 * width * ranks, transcendentals=0
            ),
            name="low_products",
        )(*xs, down_maps)
        pieces = [swap(piece, 0, j) if j else piece for j, piece in enumerate(pieces)]
        step = 512 if columns % 512 == 0 else columns
        base = pl.pallas_call(
            functools.partial(base_kernel, count),
            grid=(columns // step,),
            out_shape=shape((part_rows, columns), F32),
            in_specs=[pl.BlockSpec((GROUP_ROWS, width + LANES), lambda i: (0, 0))] * count
            + [pl.BlockSpec((width, step), lambda i: (0, i))],
            out_specs=pl.BlockSpec((part_rows, step), lambda i: (0, i)),
            compiler_params=PARAMS,
            cost_estimate=pl.CostEstimate(
                flops=2 * part_rows * width * columns, bytes_accessed=2 * width * columns, transcendentals=0
            ),
            name="base_products",
        )(*xs, weight)
        shares = pl.pallas_call(
            functools.partial(up_kernel, count, tensor_count, adapters),
            out_shape=[shape((GROUP_ROWS, block), BF16)] * (count * tensor_count),
            in_specs=[VMEM] * (3 + tensor_count),
            out_specs=[VMEM] * (count * tensor_count),
            scratch_shapes=[pltpu.VMEM((2, adapters * portion, part_rows), F32)],
            compiler_params=PARAMS,
            name="up_products",
        )(base, tags, up_flat, *pieces)
        if store_count * tensor_count <= 16:
            for g, k in enumerate(part):
                received[k] = [
                    swap(shares[g * tensor_count + j], k, j) if k or j else shares[g * tensor_count + j]
                    for j in range(tensor_count)
                ]
        else:
            me = lax.axis_index("tensor")
            order = jnp.arange(tensor_count, dtype=jnp.int32) ^ me
            for g, k in enumerate(part):
                stacked = jnp.stack(shares[g * tensor_count : (g + 1) * tensor_count])
                stacked = jnp.take(stacked, order, axis=0)
                summed = lax.all_to_all(stacked, "tensor", 0, 0, tiled=True).astype(F32).sum(0).astype(BF16)
                received[k] = [swap(summed, k, 0) if k else summed]

    counts = tuple(len(received[k]) for k in range(store_count))
    return pl.pallas_call(
        functools.partial(finish_kernel, counts),
        out_shape=shape((rows, block), BF16),
        in_specs=[VMEM] * (1 + sum(counts)),
        out_specs=VMEM,
        scratch_shapes=[pltpu.VMEM((store_count * GROUP_ROWS, block), BF16)],
        compiler_params=PARAMS,
        name="finish",
    )(place, *[value for k in range(store_count) for value in received[k]])


def solution(mesh):
    in_specs = (
        P(("groups", "store"), "tensor"),
        P("tensor", None),
        P(("groups", "store"), "tensor", None),
        P(("groups", "store"), "tensor", None),
        P(("groups", "store")),
        P(("groups", "store")),
    )
    out_specs = P(("groups", "store"), "tensor")
    return jax.shard_map(shards, mesh=mesh, in_specs=in_specs, out_specs=out_specs, check_vma=False)
```

time: 174 us -> 76 us (0.44)
  waiting for transfers between devices: 89.2 us -> 18.4 us
  blocking collectives: 29.4 us -> 0 us
  starting transfers between devices: 8.5 us -> 35 us
  Pallas kernels: 0 us -> 19.6 us
  between operations: 13.5 us -> 0.1 us
  matrix products: 11.2 us -> 0 us
  local copies, waits for them, and re-layouts: 13.7 us -> 2.58 us
  other arithmetic: 8.28 us -> 0 us
    all_to_all x2 -> x0, waiting for transfers between devices: 46.6 us -> none  [the longest x1 46.6 us: shards(): lax.all_to_all(down_row_block, 'store', split_axis=0, concat_axis=0, tile...]
    reduce_scatter x1 -> x0, waiting for transfers between devices: 42.5 us -> none  [shards(): lax.psum_scatter(partials, 'tensor', scatter_dimension=1, tiled=True)]
    ppermute x0 -> x24, starting transfers between devices: none -> 35 us  [swap(): return lax.ppermute(value, ('store', 'tensor'), pairs)]
    psum x1 -> x0, blocking collectives: 21.6 us -> none  [shards(): low_rank = lax.psum(low_part, 'tensor').astype(jnp.bfloat16)]
    pallas_call x0 -> x8, Pallas kernels: none -> 19.6 us  [the longest x2 11.8 us: shards(): pl.pallas_call(functools.partial(base_kernel, count), grid=(columns // st...]
    ppermute x0 -> x24, waiting for transfers between devices: none -> 18.4 us  [swap(): return lax.ppermute(value, ('store', 'tensor'), pairs)]
    gather x3 -> x0, local copies, waits for them, and re-layouts: 13.2 us -> none  [the longest x2 12.7 us: shards(): down_row_block = jnp.take(adapter_down_maps, requested_ids, axis=0)]
    dot_general x4 -> x0, matrix products: 11.2 us -> none  [the longest x1 7.09 us: shards(): jnp.dot(tokens, key_value_weight, preferred_element_type=jnp.float32)]
  transfers between devices with their start and end apart: 3 -> 24, of which waited for: 2 -> 6; matrix products, arithmetic and copies ran while one was open for 3% -> 0% of each run, Pallas kernels for 0% -> 23%
where the time goes in v1:
time: 76 us; the launch traced here: 75.7 us
  starting transfers between devices  35 us (46%)
  Pallas kernels  19.6 us (26%)
  waiting for transfers between devices  18.4 us (24%)
  local copies, waits for them, and re-layouts  2.58 us (3%)
    ppermute x24, starting transfers between devices, swap(): return lax.ppermute(value, ('store', 'tensor'), pairs)  35 us
    ppermute x24, waiting for transfers between devices, swap(): return lax.ppermute(value, ('store', 'tensor'), pairs)  18.4 us
    pallas_call x2, Pallas kernels, shards(): pl.pallas_call(functools.partial(base_kernel, count), grid=(columns // st...  11.8 us
    pallas_call x2, Pallas kernels, shards(): pl.pallas_call(functools.partial(down_kernel, count, tensor_count), out_s...  4.87 us
    unnamed x8, local copies, waits for them, and re-layouts  2.58 us
  transfers between devices with their start and end apart: 24, of which 6 were waited for; matrix products, arithmetic and copies ran while one was open for 0% of the time, Pallas kernels for 23%

profile of v1, /device:TPU:0, one launch (start us, length us, event | category | flops | bytes accessed | tf_op | source)
XLA Modules:
  0.0 75.7 jit_solution(12372322166630505942)
XLA Ops:
  0.0 0.0 copy-start.1
  0.0 1.2 %copy-done.1 = bf16[256,2048]{1,0:T(8,128)(2,1)S(1)} copy-done((bf16[256,2048]{1,0:T(8,128)(2,1)S(1)}, bf16[256,2048]{1,0:T(8,128)(2,1)}, u32[]{:S(2)}) %copy-start.1) | copy-done | bytes 1048600
  1.2 0.0 copy-start.2
  1.2 0.7 copy-done.2
  1.9 0.0 copy-start.3
  1.9 0.7 copy-done.3
  2.6 1.1 %group_rows.1 = (bf16[256,256]{1,0:T(8,128)(2,1)S(1)}, bf16[64,2176]{1,0:T(8,128)(2,1)S(1)}, bf16[64,2176]{1,0:T(8,128)(2,1)S(1)}, bf16[64,2176]{1,0:T(8,128)(2,1)S(1)}, bf16[64,2176]{1,0:T(8,128)(2,1)S(1)}) custom-call(s32[1,256]{1,0:T(1,128)S(1)} %bitcast.5, s32[1,256]{1,0:T(1,128)S(1)} %bitcast.6, bf16[256,2048]{1,0:T(8,128)(2,1)S(1)} %copy-done.1), custom_call_target="tpu_custom_call" | custom-call | tf_op jit(solution)/shard_map/group_rows/pallas_call | solution.py:145
  3.7 3.0 %collective-permute-start.11 = (bf16[64,2176]{1,0:T(8,128)(2,1)S(1)}, bf16[64,2176]{1,0:T(8,128)(2,1)S(1)}, u32[]{:S(2)}, u32[]{:S(2)}) collective-permute-start(bf16[64,2176]{1,0:T(8,128)(2,1)S(1)} %get-tuple-element.52), channel_id=1, source_target_pairs={{0,8},{1,9},{2,10},{3,11},{4,12},{5,13},{6,14},{7,15},{8,0},{9,1},... | collective-permute-start | bytes 835592 | tf_op jit(solution)/shard_map/ppermute | solution.py:143
  6.7 0.0 collective-permute-start.12
  6.7 0.2 collective-permute-start
  6.9 7.3 %collective-permute-done.11.refs_0_ = bf16[64,2176]{1,0:T(8,128)(2,1)S(1)} collective-permute-done((bf16[64,2176]{1,0:T(8,128)(2,1)S(1)}, bf16[64,2176]{1,0:T(8,128)(2,1)S(1)}, u32[]{:S(2)}, u32[]{:S(2)}) %collective-permute-start.11) | collective-permute-done | bytes 278560 | tf_op jit(solution)/shard_map/ppermute | solution.py:143
  14.2 4.4 %collective-permute-done.12.refs_1_ = bf16[64,2176]{1,0:T(8,128)(2,1)S(1)} collective-permute-done((bf16[64,2176]{1,0:T(8,128)(2,1)S(1)}, bf16[64,2176]{1,0:T(8,128)(2,1)S(1)}, u32[]{:S(2)}, u32[]{:S(2)}) %collective-permute-start.12) | collective-permute-done | bytes 278560 | tf_op jit(solution)/shard_map/ppermute | solution.py:143
  18.6 2.4 %low_products.3 = (f32[8,128]{1,0:T(8,128)S(1)}, f32[32,128]{1,0:T(8,128)S(1)}, f32[32,128]{1,0:T(8,128)S(1)}, f32[32,128]{1,0:T(8,128)S(1)}, f32[32,128]{1,0:T(8,128)S(1)}) custom-call(bf16[64,2176]{1,0:T(8,128)(2,1)S(1)} %collective-permute-done.11.refs_0_, bf16[64,2176]{1,0:T(8,128)(2,1)S(1)} %collective-permute-done.12.refs_1_, ...), custom_call_target="tpu_custom_call" | custom-call | flops 134217728 | bytes 2097152 | tf_op jit(solution)/shard_map/low_products/pallas_call | solution.py:171
  21.0 1.6 %collective-permute-start.13 = (f32[32,128]{1,0:T(8,128)S(1)}, f32[32,128]{1,0:T(8,128)S(1)}, u32[]{:S(2)}, u32[]{:S(2)}) collective-permute-start(f32[32,128]{1,0:T(8,128)S(1)} %get-tuple-element.56), channel_id=1, source_target_pairs={{0,1},{1,0},{2,3},{3,2},{4,5},{5,4},{6,7},{7,6},{8,9},{9,8},{10,11... | collective-permute-start | bytes 49160 | tf_op jit(solution)/shard_map/ppermute | solution.py:143
  22.6 2.6 %collective-permute-start.14 = (f32[32,128]{1,0:T(8,128)S(1)}, f32[32,128]{1,0:T(8,128)S(1)}, u32[]{:S(2)}, u32[]{:S(2)}) collective-permute-start(f32[32,128]{1,0:T(8,128)S(1)} %get-tuple-element.57), channel_id=1, source_target_pairs={{0,2},{1,3},{2,0},{3,1},{4,6},{5,7},{6,4},{7,5},{8,10},{9,11},{10,... | collective-permute-start | bytes 49160 | tf_op jit(solution)/shard_map/ppermute | solution.py:143
  25.2 0.2 collective-permute-start.15
  25.4 0.0 collective-permute-done.refs_1_
  25.4 0.0 copy-start
  25.4 2.5 %low_products.2 = (f32[8,128]{1,0:T(8,128)S(1)}, f32[32,128]{1,0:T(8,128)S(1)}, f32[32,128]{1,0:T(8,128)S(1)}, f32[32,128]{1,0:T(8,128)S(1)}, f32[32,128]{1,0:T(8,128)S(1)}) custom-call(bf16[64,2176]{1,0:T(8,128)(2,1)S(1)} %get-tuple-element.37.refs_0_, bf16[64,2176]{1,0:T(8,128)(2,1)S(1)} %collective-permute-done.refs_1_, bf16[16,2048,128]{2,1,0:T(8,128)(2,1)} %refs_2_.7), custom_call_target="tpu_custom_call" | custom-call | flops 134217728 | bytes 2097152 | tf_op jit(solution)/shard_map/low_products/pallas_call | solution.py:171
  27.9 0.7 collective-permute-start.1
  28.6 3.5 %collective-permute-start.2 = (f32[32,128]{1,0:T(8,128)S(1)}, f32[32,128]{1,0:T(8,128)S(1)}, u32[]{:S(2)}, u32[]{:S(2)}) collective-permute-start(f32[32,128]{1,0:T(8,128)S(1)} %get-tuple-element.42), channel_id=1, source_target_pairs={{0,2},{1,3},{2,0},{3,1},{4,6},{5,7},{6,4},{7,5},{8,10},{9,11},{10,... | collective-permute-start | bytes 49160 | tf_op jit(solution)/shard_map/ppermute | solution.py:143
  32.1 0.0 collective-permute-done.13.refs_1_
  32.1 0.2 collective-permute-start.3
  32.4 5.9 %base_products.3.base_ref = f32[128,2048]{1,0:T(8,128)S(1)} custom-call(bf16[64,2176]{1,0:T(8,128)(2,1)S(1)} %collective-permute-done.11.refs_0_, bf16[64,2176]{1,0:T(8,128)(2,1)S(1)} %collective-permute-done.12.refs_1_, bf16[2048,2048]{1,0:T(8,128)(2,1)} %refs_2_.6), custom_call_target="tpu_custom_call" | custom-call | flops 1073741824 | bytes 8388608 | tf_op jit(solution)/shard_map/base_products/pallas_call | solution.py:190
  38.3 0.0 collective-permute-done.14.refs_2_
  38.3 0.0 collective-permute-done.15.refs_3_
  38.3 0.0 copy-done
  38.3 0.4 up_products.3
  38.7 1.4 %collective-permute-start.16 = (bf16[64,512]{1,0:T(8,128)(2,1)S(1)}, bf16[64,512]{1,0:T(8,128)(2,1)S(1)}, u32[]{:S(2)}, u32[]{:S(2)}) collective-permute-start(bf16[64,512]{1,0:T(8,128)(2,1)S(1)} %get-tuple-element.59), channel_id=1, source_target_pairs={{0,8},{1,9},{2,10},{3,11},{4,12},{5,13},{6,14},{7,15},{8,0},{9,1},... | collective-permute-start | bytes 196616 | tf_op jit(solution)/shard_map/ppermute | solution.py:143
  40.1 0.5 collective-permute-start.17
  40.6 0.0 collective-permute-done.1.refs_1_
  40.6 4.6 %collective-permute-start.18 = (bf16[64,512]{1,0:T(8,128)(2,1)S(1)}, bf16[64,512]{1,0:T(8,128)(2,1)S(1)}, u32[]{:S(2)}, u32[]{:S(2)}) collective-permute-start(bf16[64,512]{1,0:T(8,128)(2,1)S(1)} %get-tuple-element.61), channel_id=1, source_target_pairs={{0,10},{1,11},{2,8},{3,9},{4,14},{5,15},{6,12},{7,13},{8,2},{9,3},... | collective-permute-start | bytes 196616 | tf_op jit(solution)/shard_map/ppermute | solution.py:143
  45.2 0.0 collective-permute-done.2.refs_2_
  45.2 0.4 collective-permute-start.19
  45.5 0.0 collective-permute-done.3.refs_3_
  45.5 0.0 collective-permute-start.20
  45.5 5.9 %base_products.2.base_ref = f32[128,2048]{1,0:T(8,128)S(1)} custom-call(bf16[64,2176]{1,0:T(8,128)(2,1)S(1)} %get-tuple-element.37.refs_0_, bf16[64,2176]{1,0:T(8,128)(2,1)S(1)} %collective-permute-done.refs_1_, bf16[2048,2048]{1,0:T(8,128)(2,1)} %refs_2_.6), custom_call_target="tpu_custom_call" | custom-call | flops 1073741824 | bytes 8388608 | tf_op jit(solution)/shard_map/base_products/pallas_call | solution.py:190
  51.5 0.4 up_products.2
  51.9 0.0 collective-permute-done.16.refs_8_
  51.9 1.5 %collective-permute-start.21 = (bf16[64,512]{1,0:T(8,128)(2,1)S(1)}, bf16[64,512]{1,0:T(8,128)(2,1)S(1)}, u32[]{:S(2)}, u32[]{:S(2)}) collective-permute-start(bf16[64,512]{1,0:T(8,128)(2,1)S(1)} %get-tuple-element.64), channel_id=1, source_target_pairs={{0,13},{1,12},{2,15},{3,14},{4,9},{5,8},{6,11},{7,10},{8,5},{9,4},... | collective-permute-start | bytes 196616 | tf_op jit(solution)/shard_map/ppermute | solution.py:143
  53.4 0.0 collective-permute-done.17.refs_9_
  53.4 3.3 %collective-permute-start.22 = (bf16[64,512]{1,0:T(8,128)(2,1)S(1)}, bf16[64,512]{1,0:T(8,128)(2,1)S(1)}, u32[]{:S(2)}, u32[]{:S(2)}) collective-permute-start(bf16[64,512]{1,0:T(8,128)(2,1)S(1)} %get-tuple-element.65), channel_id=1, source_target_pairs={{0,14},{1,15},{2,12},{3,13},{4,10},{5,11},{6,8},{7,9},{8,6},{9,7},... | collective-permute-start | bytes 196616 | tf_op jit(solution)/shard_map/ppermute | solution.py:143
  56.7 0.0 collective-permute-done.18.refs_10_
  56.7 1.4 %collective-permute-start.23 = (bf16[64,512]{1,0:T(8,128)(2,1)S(1)}, bf16[64,512]{1,0:T(8,128)(2,1)S(1)}, u32[]{:S(2)}, u32[]{:S(2)}) collective-permute-start(bf16[64,512]{1,0:T(8,128)(2,1)S(1)} %get-tuple-element.66), channel_id=1, source_target_pairs={{0,15},{1,14},{2,13},{3,12},{4,11},{5,10},{6,9},{7,8},{8,7},{9,6},... | collective-permute-start | bytes 196616 | tf_op jit(solution)/shard_map/ppermute | solution.py:143
  58.1 0.0 collective-permute-done.19.refs_11_
  58.1 2.9 %collective-permute-start.10 = (bf16[64,512]{1,0:T(8,128)(2,1)S(1)}, bf16[64,512]{1,0:T(8,128)(2,1)S(1)}, u32[]{:S(2)}, u32[]{:S(2)}) collective-permute-start(bf16[64,512]{1,0:T(8,128)(2,1)S(1)} %get-tuple-element.51), channel_id=1, source_target_pairs={{0,7},{1,6},{2,5},{3,4},{4,3},{5,2},{6,1},{7,0},{8,15},{9,14},{10,... | collective-permute-start | bytes 196616 | tf_op jit(solution)/shard_map/ppermute | solution.py:143
  61.0 0.0 collective-permute-done.20.refs_12_
  61.0 0.0 collective-permute-start.4
  61.0 0.0 collective-permute-done.21.refs_13_
  61.1 1.3 %collective-permute-start.5 = (bf16[64,512]{1,0:T(8,128)(2,1)S(1)}, bf16[64,512]{1,0:T(8,128)(2,1)S(1)}, u32[]{:S(2)}, u32[]{:S(2)}) collective-permute-start(bf16[64,512]{1,0:T(8,128)(2,1)S(1)} %get-tuple-element.46), channel_id=1, source_target_pairs={{0,2},{1,3},{2,0},{3,1},{4,6},{5,7},{6,4},{7,5},{8,10},{9,11},{10,... | collective-permute-start | bytes 196616 | tf_op jit(solution)/shard_map/ppermute | solution.py:143
  62.4 0.0 collective-permute-done.22.refs_14_
  62.4 3.1 %collective-permute-start.6 = (bf16[64,512]{1,0:T(8,128)(2,1)S(1)}, bf16[64,512]{1,0:T(8,128)(2,1)S(1)}, u32[]{:S(2)}, u32[]{:S(2)}) collective-permute-start(bf16[64,512]{1,0:T(8,128)(2,1)S(1)} %get-tuple-element.47), channel_id=1, source_target_pairs={{0,3},{1,2},{2,1},{3,0},{4,7},{5,6},{6,5},{7,4},{8,11},{9,10},{10,... | collective-permute-start | bytes 196616 | tf_op jit(solution)/shard_map/ppermute | solution.py:143
  65.4 0.0 collective-permute-done.23.refs_15_
  65.4 0.2 collective-permute-start.7
  65.7 0.0 collective-permute-done.10.refs_7_
  65.7 1.1 %collective-permute-start.8 = (bf16[64,512]{1,0:T(8,128)(2,1)S(1)}, bf16[64,512]{1,0:T(8,128)(2,1)S(1)}, u32[]{:S(2)}, u32[]{:S(2)}) collective-permute-start(bf16[64,512]{1,0:T(8,128)(2,1)S(1)} %get-tuple-element.49), channel_id=1, source_target_pairs={{0,5},{1,4},{2,7},{3,6},{4,1},{5,0},{6,3},{7,2},{8,13},{9,12},{10,... | collective-permute-start | bytes 196616 | tf_op jit(solution)/shard_map/ppermute | solution.py:143
  66.7 0.2 collective-permute-done.4.refs_1_
  67.0 1.3 %collective-permute-start.9 = (bf16[64,512]{1,0:T(8,128)(2,1)S(1)}, bf16[64,512]{1,0:T(8,128)(2,1)S(1)}, u32[]{:S(2)}, u32[]{:S(2)}) collective-permute-start(bf16[64,512]{1,0:T(8,128)(2,1)S(1)} %get-tuple-element.50), channel_id=1, source_target_pairs={{0,6},{1,7},{2,4},{3,5},{4,2},{5,3},{6,0},{7,1},{8,14},{9,15},{10,... | collective-permute-start | bytes 196616 | tf_op jit(solution)/shard_map/ppermute | solution.py:143
  68.2 2.4 %collective-permute-done.5.refs_2_ = bf16[64,512]{1,0:T(8,128)(2,1)S(1)} collective-permute-done((bf16[64,512]{1,0:T(8,128)(2,1)S(1)}, bf16[64,512]{1,0:T(8,128)(2,1)S(1)}, u32[]{:S(2)}, u32[]{:S(2)}) %collective-permute-start.5) | collective-permute-done | bytes 65568 | tf_op jit(solution)/shard_map/ppermute | solution.py:143
  70.7 0.0 collective-permute-done.6.refs_3_
  70.7 0.0 collective-permute-done.7.refs_4_
  70.7 1.2 %collective-permute-done.8.refs_5_ = bf16[64,512]{1,0:T(8,128)(2,1)S(1)} collective-permute-done((bf16[64,512]{1,0:T(8,128)(2,1)S(1)}, bf16[64,512]{1,0:T(8,128)(2,1)S(1)}, u32[]{:S(2)}, u32[]{:S(2)}) %collective-permute-start.8) | collective-permute-done | bytes 65568 | tf_op jit(solution)/shard_map/ppermute | solution.py:143
  71.9 2.7 %collective-permute-done.9.refs_6_ = bf16[64,512]{1,0:T(8,128)(2,1)S(1)} collective-permute-done((bf16[64,512]{1,0:T(8,128)(2,1)S(1)}, bf16[64,512]{1,0:T(8,128)(2,1)S(1)}, u32[]{:S(2)}, u32[]{:S(2)}) %collective-permute-start.9) | collective-permute-done | bytes 65568 | tf_op jit(solution)/shard_map/ppermute | solution.py:143
  74.7 1.0 %finish.1 = bf16[256,512]{1,0:T(8,128)(2,1)} custom-call(bf16[256,256]{1,0:T(8,128)(2,1)S(1)} %get-tuple-element.36.place_ref, bf16[64,512]{1,0:T(8,128)(2,1)S(1)} %get-tuple-element.44.refs_0_, bf16[64,512]{1,0:T(8,128)(2,1)S(1)} %collective-permute-done.4.refs_1_, bf16[64,512]{1,0:T(8,128)(2,1)S(1)} %collective-permute-done.5.refs_2_, ...), custom_call_target="tpu_custom_call" | custom-call | tf_op jit(solution)/shard_map/finish/pallas_call | solution.py:228
Async XLA Ops:
  0.0 1.2 %copy-start.1 = (bf16[256,2048]{1,0:T(8,128)(2,1)S(1)}, bf16[256,2048]{1,0:T(8,128)(2,1)}, u32[]{:S(2)}) copy-start(bf16[256,2048]{1,0:T(8,128)(2,1)} %tokens_ref.1) | copy-start | bytes 3145732
  1.2 0.7 copy-start.2
  1.9 0.7 copy-start.3
  3.7 10.5 %collective-permute-start.11 = (bf16[64,2176]{1,0:T(8,128)(2,1)S(1)}, bf16[64,2176]{1,0:T(8,128)(2,1)S(1)}, u32[]{:S(2)}, u32[]{:S(2)}) collective-permute-start(bf16[64,2176]{1,0:T(8,128)(2,1)S(1)} %get-tuple-element.52), channel_id=1, source_target_pairs={{0,8},{1,9},{2,10},{3,11},{4,12},{5,13},{6,14},{7,15},{8,0},{9,1},... | collective-permute-start | bytes 835592 | tf_op jit(solution)/shard_map/ppermute | solution.py:143
  6.7 11.9 %collective-permute-start.12 = (bf16[64,2176]{1,0:T(8,128)(2,1)S(1)}, bf16[64,2176]{1,0:T(8,128)(2,1)S(1)}, u32[]{:S(2)}, u32[]{:S(2)}) collective-permute-start(bf16[64,2176]{1,0:T(8,128)(2,1)S(1)} %get-tuple-element.53), channel_id=1, source_target_pairs={{0,12},{1,13},{2,14},{3,15},{4,8},{5,9},{6,10},{7,11},{8,4},{9,5},... | collective-permute-start | bytes 835592 | tf_op jit(solution)/shard_map/ppermute | solution.py:143
  6.7 18.7 %collective-permute-start = (bf16[64,2176]{1,0:T(8,128)(2,1)S(1)}, bf16[64,2176]{1,0:T(8,128)(2,1)S(1)}, u32[]{:S(2)}, u32[]{:S(2)}) collective-permute-start(bf16[64,2176]{1,0:T(8,128)(2,1)S(1)} %get-tuple-element.38), channel_id=1, source_target_pairs={{0,4},{1,5},{2,6},{3,7},{4,0},{5,1},{6,2},{7,3},{8,12},{9,13},{10,... | collective-permute-start | bytes 835592 | tf_op jit(solution)/shard_map/ppermute | solution.py:143
  21.0 11.2 %collective-permute-start.13 = (f32[32,128]{1,0:T(8,128)S(1)}, f32[32,128]{1,0:T(8,128)S(1)}, u32[]{:S(2)}, u32[]{:S(2)}) collective-permute-start(f32[32,128]{1,0:T(8,128)S(1)} %get-tuple-element.56), channel_id=1, source_target_pairs={{0,1},{1,0},{2,3},{3,2},{4,5},{5,4},{6,7},{7,6},{8,9},{9,8},{10,11... | collective-permute-start | bytes 49160 | tf_op jit(solution)/shard_map/ppermute | solution.py:143
  22.6 15.7 %collective-permute-start.14 = (f32[32,128]{1,0:T(8,128)S(1)}, f32[32,128]{1,0:T(8,128)S(1)}, u32[]{:S(2)}, u32[]{:S(2)}) collective-permute-start(f32[32,128]{1,0:T(8,128)S(1)} %get-tuple-element.57), channel_id=1, source_target_pairs={{0,2},{1,3},{2,0},{3,1},{4,6},{5,7},{6,4},{7,5},{8,10},{9,11},{10,... | collective-permute-start | bytes 49160 | tf_op jit(solution)/shard_map/ppermute | solution.py:143
  25.2 13.1 %collective-permute-start.15 = (f32[32,128]{1,0:T(8,128)S(1)}, f32[32,128]{1,0:T(8,128)S(1)}, u32[]{:S(2)}, u32[]{:S(2)}) collective-permute-start(f32[32,128]{1,0:T(8,128)S(1)} %get-tuple-element.58), channel_id=1, source_target_pairs={{0,3},{1,2},{2,1},{3,0},{4,7},{5,6},{6,5},{7,4},{8,11},{9,10},{10,... | collective-permute-start | bytes 49160 | tf_op jit(solution)/shard_map/ppermute | solution.py:143
  25.4 12.9 %copy-start = (bf16[16,16,2048]{2,1,0:T(8,128)(2,1)S(1)}, bf16[16,16,2048]{2,1,0:T(8,128)(2,1)}, u32[]{:S(2)}) copy-start(bf16[16,16,2048]{2,1,0:T(8,128)(2,1)} %param.9) | copy-start | bytes 3145732
  27.9 12.7 %collective-permute-start.1 = (f32[32,128]{1,0:T(8,128)S(1)}, f32[32,128]{1,0:T(8,128)S(1)}, u32[]{:S(2)}, u32[]{:S(2)}) collective-permute-start(f32[32,128]{1,0:T(8,128)S(1)} %get-tuple-element.41), channel_id=1, source_target_pairs={{0,1},{1,0},{2,3},{3,2},{4,5},{5,4},{6,7},{7,6},{8,9},{9,8},{10,11... | collective-permute-start | bytes 49160 | tf_op jit(solution)/shard_map/ppermute | solution.py:143
  28.6 16.5 %collective-permute-start.2 = (f32[32,128]{1,0:T(8,128)S(1)}, f32[32,128]{1,0:T(8,128)S(1)}, u32[]{:S(2)}, u32[]{:S(2)}) collective-permute-start(f32[32,128]{1,0:T(8,128)S(1)} %get-tuple-element.42), channel_id=1, source_target_pairs={{0,2},{1,3},{2,0},{3,1},{4,6},{5,7},{6,4},{7,5},{8,10},{9,11},{10,... | collective-permute-start | bytes 49160 | tf_op jit(solution)/shard_map/ppermute | solution.py:143
  32.1 13.4 %collective-permute-start.3 = (f32[32,128]{1,0:T(8,128)S(1)}, f32[32,128]{1,0:T(8,128)S(1)}, u32[]{:S(2)}, u32[]{:S(2)}) collective-permute-start(f32[32,128]{1,0:T(8,128)S(1)} %get-tuple-element.43), channel_id=1, source_target_pairs={{0,3},{1,2},{2,1},{3,0},{4,7},{5,6},{6,5},{7,4},{8,11},{9,10},{10,... | collective-permute-start | bytes 49160 | tf_op jit(solution)/shard_map/ppermute | solution.py:143
  38.7 13.2 %collective-permute-start.16 = (bf16[64,512]{1,0:T(8,128)(2,1)S(1)}, bf16[64,512]{1,0:T(8,128)(2,1)S(1)}, u32[]{:S(2)}, u32[]{:S(2)}) collective-permute-start(bf16[64,512]{1,0:T(8,128)(2,1)S(1)} %get-tuple-element.59), channel_id=1, source_target_pairs={{0,8},{1,9},{2,10},{3,11},{4,12},{5,13},{6,14},{7,15},{8,0},{9,1},... | collective-permute-start | bytes 196616 | tf_op jit(solution)/shard_map/ppermute | solution.py:143
  40.1 13.3 %collective-permute-start.17 = (bf16[64,512]{1,0:T(8,128)(2,1)S(1)}, bf16[64,512]{1,0:T(8,128)(2,1)S(1)}, u32[]{:S(2)}, u32[]{:S(2)}) collective-permute-start(bf16[64,512]{1,0:T(8,128)(2,1)S(1)} %get-tuple-element.60), channel_id=1, source_target_pairs={{0,9},{1,8},{2,11},{3,10},{4,13},{5,12},{6,15},{7,14},{8,1},{9,0},... | collective-permute-start | bytes 196616 | tf_op jit(solution)/shard_map/ppermute | solution.py:143
  40.6 16.2 %collective-permute-start.18 = (bf16[64,512]{1,0:T(8,128)(2,1)S(1)}, bf16[64,512]{1,0:T(8,128)(2,1)S(1)}, u32[]{:S(2)}, u32[]{:S(2)}) collective-permute-start(bf16[64,512]{1,0:T(8,128)(2,1)S(1)} %get-tuple-element.61), channel_id=1, source_target_pairs={{0,10},{1,11},{2,8},{3,9},{4,14},{5,15},{6,12},{7,13},{8,2},{9,3},... | collective-permute-start | bytes 196616 | tf_op jit(solution)/shard_map/ppermute | solution.py:143
  45.2 13.0 %collective-permute-start.19 = (bf16[64,512]{1,0:T(8,128)(2,1)S(1)}, bf16[64,512]{1,0:T(8,128)(2,1)S(1)}, u32[]{:S(2)}, u32[]{:S(2)}) collective-permute-start(bf16[64,512]{1,0:T(8,128)(2,1)S(1)} %get-tuple-element.62), channel_id=1, source_target_pairs={{0,11},{1,10},{2,9},{3,8},{4,15},{5,14},{6,13},{7,12},{8,3},{9,2},... | collective-permute-start | bytes 196616 | tf_op jit(solution)/shard_map/ppermute | solution.py:143
  45.5 15.5 %collective-permute-start.20 = (bf16[64,512]{1,0:T(8,128)(2,1)S(1)}, bf16[64,512]{1,0:T(8,128)(2,1)S(1)}, u32[]{:S(2)}, u32[]{:S(2)}) collective-permute-start(bf16[64,512]{1,0:T(8,128)(2,1)S(1)} %get-tuple-element.63), channel_id=1, source_target_pairs={{0,12},{1,13},{2,14},{3,15},{4,8},{5,9},{6,10},{7,11},{8,4},{9,5},... | collective-permute-start | bytes 196616 | tf_op jit(solution)/shard_map/ppermute | solution.py:143
  51.9 9.2 %collective-permute-start.21 = (bf16[64,512]{1,0:T(8,128)(2,1)S(1)}, bf16[64,512]{1,0:T(8,128)(2,1)S(1)}, u32[]{:S(2)}, u32[]{:S(2)}) collective-permute-start(bf16[64,512]{1,0:T(8,128)(2,1)S(1)} %get-tuple-element.64), channel_id=1, source_target_pairs={{0,13},{1,12},{2,15},{3,14},{4,9},{5,8},{6,11},{7,10},{8,5},{9,4},... | collective-permute-start | bytes 196616 | tf_op jit(solution)/shard_map/ppermute | solution.py:143
  53.4 9.0 %collective-permute-start.22 = (bf16[64,512]{1,0:T(8,128)(2,1)S(1)}, bf16[64,512]{1,0:T(8,128)(2,1)S(1)}, u32[]{:S(2)}, u32[]{:S(2)}) collective-permute-start(bf16[64,512]{1,0:T(8,128)(2,1)S(1)} %get-tuple-element.65), channel_id=1, source_target_pairs={{0,14},{1,15},{2,12},{3,13},{4,10},{5,11},{6,8},{7,9},{8,6},{9,7},... | collective-permute-start | bytes 196616 | tf_op jit(solution)/shard_map/ppermute | solution.py:143
  56.7 8.7 %collective-permute-start.23 = (bf16[64,512]{1,0:T(8,128)(2,1)S(1)}, bf16[64,512]{1,0:T(8,128)(2,1)S(1)}, u32[]{:S(2)}, u32[]{:S(2)}) collective-permute-start(bf16[64,512]{1,0:T(8,128)(2,1)S(1)} %get-tuple-element.66), channel_id=1, source_target_pairs={{0,15},{1,14},{2,13},{3,12},{4,11},{5,10},{6,9},{7,8},{8,7},{9,6},... | collective-permute-start | bytes 196616 | tf_op jit(solution)/shard_map/ppermute | solution.py:143
  58.1 7.6 %collective-permute-start.10 = (bf16[64,512]{1,0:T(8,128)(2,1)S(1)}, bf16[64,512]{1,0:T(8,128)(2,1)S(1)}, u32[]{:S(2)}, u32[]{:S(2)}) collective-permute-start(bf16[64,512]{1,0:T(8,128)(2,1)S(1)} %get-tuple-element.51), channel_id=1, source_target_pairs={{0,7},{1,6},{2,5},{3,4},{4,3},{5,2},{6,1},{7,0},{8,15},{9,14},{10,... | collective-permute-start | bytes 196616 | tf_op jit(solution)/shard_map/ppermute | solution.py:143
  61.0 5.9 %collective-permute-start.4 = (bf16[64,512]{1,0:T(8,128)(2,1)S(1)}, bf16[64,512]{1,0:T(8,128)(2,1)S(1)}, u32[]{:S(2)}, u32[]{:S(2)}) collective-permute-start(bf16[64,512]{1,0:T(8,128)(2,1)S(1)} %get-tuple-element.45), channel_id=1, source_target_pairs={{0,1},{1,0},{2,3},{3,2},{4,5},{5,4},{6,7},{7,6},{8,9},{9,8},{10,11... | collective-permute-start | bytes 196616 | tf_op jit(solution)/shard_map/ppermute | solution.py:143
  61.1 9.6 %collective-permute-start.5 = (bf16[64,512]{1,0:T(8,128)(2,1)S(1)}, bf16[64,512]{1,0:T(8,128)(2,1)S(1)}, u32[]{:S(2)}, u32[]{:S(2)}) collective-permute-start(bf16[64,512]{1,0:T(8,128)(2,1)S(1)} %get-tuple-element.46), channel_id=1, source_target_pairs={{0,2},{1,3},{2,0},{3,1},{4,6},{5,7},{6,4},{7,5},{8,10},{9,11},{10,... | collective-permute-start | bytes 196616 | tf_op jit(solution)/shard_map/ppermute | solution.py:143
  62.4 8.3 %collective-permute-start.6 = (bf16[64,512]{1,0:T(8,128)(2,1)S(1)}, bf16[64,512]{1,0:T(8,128)(2,1)S(1)}, u32[]{:S(2)}, u32[]{:S(2)}) collective-permute-start(bf16[64,512]{1,0:T(8,128)(2,1)S(1)} %get-tuple-element.47), channel_id=1, source_target_pairs={{0,3},{1,2},{2,1},{3,0},{4,7},{5,6},{6,5},{7,4},{8,11},{9,10},{10,... | collective-permute-start | bytes 196616 | tf_op jit(solution)/shard_map/ppermute | solution.py:143
  65.4 5.3 %collective-permute-start.7 = (bf16[64,512]{1,0:T(8,128)(2,1)S(1)}, bf16[64,512]{1,0:T(8,128)(2,1)S(1)}, u32[]{:S(2)}, u32[]{:S(2)}) collective-permute-start(bf16[64,512]{1,0:T(8,128)(2,1)S(1)} %get-tuple-element.48), channel_id=1, source_target_pairs={{0,4},{1,5},{2,6},{3,7},{4,0},{5,1},{6,2},{7,3},{8,12},{9,13},{10,... | collective-permute-start | bytes 196616 | tf_op jit(solution)/shard_map/ppermute | solution.py:143
  65.7 6.3 %collective-permute-start.8 = (bf16[64,512]{1,0:T(8,128)(2,1)S(1)}, bf16[64,512]{1,0:T(8,128)(2,1)S(1)}, u32[]{:S(2)}, u32[]{:S(2)}) collective-permute-start(bf16[64,512]{1,0:T(8,128)(2,1)S(1)} %get-tuple-element.49), channel_id=1, source_target_pairs={{0,5},{1,4},{2,7},{3,6},{4,1},{5,0},{6,3},{7,2},{8,13},{9,12},{10,... | collective-permute-start | bytes 196616 | tf_op jit(solution)/shard_map/ppermute | solution.py:143
  67.0 7.7 %collective-permute-start.9 = (bf16[64,512]{1,0:T(8,128)(2,1)S(1)}, bf16[64,512]{1,0:T(8,128)(2,1)S(1)}, u32[]{:S(2)}, u32[]{:S(2)}) collective-permute-start(bf16[64,512]{1,0:T(8,128)(2,1)S(1)} %get-tuple-element.50), channel_id=1, source_target_pairs={{0,6},{1,7},{2,4},{3,5},{4,2},{5,3},{6,0},{7,1},{8,14},{9,15},{10,... | collective-permute-start | bytes 196616 | tf_op jit(solution)/shard_map/ppermute | solution.py:143

commit v2 on v1

--- a/solution.py
+++ b/solution.py
@@ -21,9 +21,20 @@
     return lax.dot_general(a, b, (((dim_a,), (dim_b,)), ((), ())), preferred_element_type=F32)
 
 
-def group_kernel(store_count, ids_ref, slots_ref, tokens_ref, *outs):
-    place_ref, group_refs = outs[0], outs[1:]
+def group_kernel(store_count, ids_hbm, slots_hbm, tokens_hbm, *outs):
+    place_ref, group_refs = outs[0], outs[1 : 1 + store_count]
+    ids_ref, slots_ref, tokens_ref, sems = outs[1 + store_count :]
     me = lax.axis_index("store")
+    copies = [
+        pltpu.make_async_copy(source, target, sems.at[i])
+        for i, (source, target) in enumerate(
+            ((slots_hbm, slots_ref), (ids_hbm, ids_ref), (tokens_hbm, tokens_ref))
+        )
+    ]
+    for copy in copies:
+        copy.start()
+    copies[0].wait()
+    copies[1].wait()
     rows, width = tokens_ref.shape
     owner = slots_ref[...] // SLOTS
     relative = owner ^ me
@@ -34,17 +45,21 @@
     rank = jnp.sum(jnp.where(mine, count, 0.0), axis=0, keepdims=True).astype(jnp.int32) - 1
     tags = jnp.broadcast_to((ids_ref[...] + 1).astype(F32), (LANES, rows)).astype(BF16)
     position = lax.broadcasted_iota(jnp.int32, (GROUP_ROWS, rows), 0)
-    for k, out in enumerate(group_refs):
+    places = []
+    for k in range(store_count):
         place = ((relative == k) & (rank == position)).astype(F32).astype(BF16)
         place_ref[k * GROUP_ROWS : (k + 1) * GROUP_ROWS, :] = place
+        places.append(place)
+    copies[2].wait()
+    for place, out in zip(places, group_refs):
         out[:, :width] = contract(place, tokens_ref[...], 1, 0).astype(BF16)
         out[:, width:] = contract(place, tags, 1, 1).astype(BF16)
 
 
-def down_kernel(group_count, tensor_count, *refs):
-    xs, down_ref = refs[:group_count], refs[group_count]
-    tags_ref, pieces = refs[group_count + 1], refs[group_count + 2 : group_count + 2 + tensor_count]
-    maps, low, low_t, sems = refs[group_count + 2 + tensor_count :]
+def down_kernel(group_count, tensor_count, after_count, *refs):
+    xs, down_ref, refs = refs[:group_count], refs[group_count], refs[group_count + 1 + after_count :]
+    tags_ref, pieces = refs[0], refs[1 : 1 + tensor_count]
+    maps, low, low_t, sems = refs[1 + tensor_count :]
     me = lax.axis_index("tensor")
     adapters, width, ranks = down_ref.shape
     copies, tops = [], []
@@ -84,8 +99,8 @@
 def base_kernel(group_count, *refs):
     xs, weight_ref, out_ref = refs[:group_count], refs[group_count], refs[group_count + 1]
     width = weight_ref.shape[0]
-    for g, x in enumerate(xs):
-        out_ref[g * GROUP_ROWS : (g + 1) * GROUP_ROWS, :] = contract(x[:, :width], weight_ref[...], 1, 0)
+    x = jnp.concatenate([x[:, :width] for x in xs], axis=0)
+    out_ref[...] = contract(x, weight_ref[...], 1, 0)
 
 
 def up_kernel(group_count, tensor_count, adapters, base_ref, tags_ref, up_ref, *refs):
@@ -108,20 +123,30 @@
         total = base_ref[:, columns] + contract(
             mixed[to // (tensor_count // 2)].astype(BF16), up_ref[:, columns], 0, 0
         )
-        for g in range(group_count):
-            outs[g * tensor_count + j][...] = total[g * GROUP_ROWS : (g + 1) * GROUP_ROWS, :].astype(BF16)
-
-
-def finish_kernel(counts, place_ref, *refs):
-    out_ref, grouped = refs[-2], refs[-1]
-    first = 0
-    for k, count in enumerate(counts):
-        total = refs[first][...].astype(F32)
-        for ref in refs[first + 1 : first + count]:
-            total = total + ref[...].astype(F32)
+        for p in range(len(outs) // tensor_count):
+            out = outs[p * tensor_count + j]
+            out[...] = total[p * out.shape[0] : (p + 1) * out.shape[0], :].astype(BF16)
+
+
+def sum_kernel(counts, *refs):
+    outs, first = refs[sum(counts) :], 0
+    for p, count in enumerate(counts):
+        for h, out in enumerate(outs):
+            rows = pl.ds(h * GROUP_ROWS, GROUP_ROWS)
+            total = refs[first][rows, :].astype(F32)
+            for ref in refs[first + 1 : first + count]:
+                total = total + ref[rows, :].astype(F32)
+            out[p * GROUP_ROWS : (p + 1) * GROUP_ROWS, :] = total.astype(BF16)
         first += count
-        grouped[k * GROUP_ROWS : (k + 1) * GROUP_ROWS, :] = total.astype(BF16)
-    out_ref[...] = contract(place_ref[...], grouped[...], 0, 0).astype(BF16)
+
+
+def finish_kernel(both, place_ref, *refs):
+    halves, out_ref = refs[:both], refs[both]
+    groups = []
+    for k in range(place_ref.shape[0] // GROUP_ROWS):
+        p = k // both
+        groups.append(halves[k % both][p * GROUP_ROWS : (p + 1) * GROUP_ROWS, :])
+    out_ref[...] = contract(place_ref[...], jnp.concatenate(groups, axis=0), 0, 0).astype(BF16)
 
 
 def shards(tokens, weight, down_maps, up_maps, local_ids, slot_index):
@@ -146,21 +171,26 @@
         functools.partial(group_kernel, store_count),
         out_shape=[shape((store_count * GROUP_ROWS, rows), BF16)]
         + [shape((GROUP_ROWS, width + LANES), BF16)] * store_count,
-        in_specs=[VMEM] * 3,
+        in_specs=[HBM] * 3,
         out_specs=[VMEM] * (store_count + 1),
+        scratch_shapes=[
+            pltpu.VMEM((1, rows), jnp.int32),
+            pltpu.VMEM((1, rows), jnp.int32),
+            pltpu.VMEM((rows, width), BF16),
+            pltpu.SemaphoreType.DMA((3,)),
+        ],
         compiler_params=PARAMS,
         name="group_rows",
     )(local_ids.reshape(1, rows), slot_index.reshape(1, rows), tokens)
 
+    both = min(2, store_count)
     far = range(2, store_count)
-    near = range(min(2, store_count))
+    near = range(both)
     arrived = {}
-    for k in far:
-        arrived[k] = swap(groups[k], k, 0)
-    for k in near:
+    for k in (*near, *far):
         arrived[k] = swap(groups[k], k, 0) if k else groups[k]
 
-    received = {}
+    received, after = [], []
     for part in (near, far):
         part = list(part)
         if not part:
@@ -169,9 +199,9 @@
         part_rows = count * GROUP_ROWS
         xs = [arrived[k] for k in part]
         tags, *pieces = pl.pallas_call(
-            functools.partial(down_kernel, count, tensor_count),
+            functools.partial(down_kernel, count, tensor_count, len(after)),
             out_shape=[shape((8, part_rows), F32)] + [shape((2 * portion, part_rows), F32)] * tensor_count,
-            in_specs=[VMEM] * count + [HBM],
+            in_specs=[VMEM] * count + [HBM] * (1 + len(after)),
             out_specs=[VMEM] * (tensor_count + 1),
             scratch_shapes=[
                 pltpu.VMEM((count, width, 2 * ranks), BF16),
@@ -184,7 +214,7 @@
                 flops=4 * part_rows * width * ranks, bytes_accessed=count * 4 * width * ranks, transcendentals=0
             ),
             name="low_products",
-        )(*xs, down_maps)
+        )(*xs, down_maps, *after)
         pieces = [swap(piece, 0, j) if j else piece for j, piece in enumerate(pieces)]
         step = 512 if columns % 512 == 0 else columns
         base = pl.pallas_call(
@@ -202,38 +232,45 @@
         )(*xs, weight)
         shares = pl.pallas_call(
             functools.partial(up_kernel, count, tensor_count, adapters),
-            out_shape=[shape((GROUP_ROWS, block), BF16)] * (count * tensor_count),
+            out_shape=[shape((both * GROUP_ROWS, block), BF16)] * (count // both * tensor_count),
             in_specs=[VMEM] * (3 + tensor_count),
-            out_specs=[VMEM] * (count * tensor_count),
+            out_specs=[VMEM] * (count // both * tensor_count),
             scratch_shapes=[pltpu.VMEM((2, adapters * portion, part_rows), F32)],
             compiler_params=PARAMS,
             name="up_products",
         )(base, tags, up_flat, *pieces)
-        if store_count * tensor_count <= 16:
-            for g, k in enumerate(part):
-                received[k] = [
-                    swap(shares[g * tensor_count + j], k, j) if k or j else shares[g * tensor_count + j]
-                    for j in range(tensor_count)
-                ]
-        else:
-            me = lax.axis_index("tensor")
-            order = jnp.arange(tensor_count, dtype=jnp.int32) ^ me
-            for g, k in enumerate(part):
-                stacked = jnp.stack(shares[g * tensor_count : (g + 1) * tensor_count])
-                stacked = jnp.take(stacked, order, axis=0)
+        after = shares[:1]
+        for p in range(count // both):
+            k = part[p * both]
+            mine = shares[p * tensor_count : (p + 1) * tensor_count]
+            if store_count * tensor_count <= 16:
+                received.append([swap(share, k, j) if k or j else share for j, share in enumerate(mine)])
+            else:
+                order = jnp.arange(tensor_count, dtype=jnp.int32) ^ lax.axis_index("tensor")
+                stacked = jnp.take(jnp.stack(mine), order, axis=0)
                 summed = lax.all_to_all(stacked, "tensor", 0, 0, tiled=True).astype(F32).sum(0).astype(BF16)
-                received[k] = [swap(summed, k, 0) if k else summed]
-
-    counts = tuple(len(received[k]) for k in range(store_count))
+                received.append([swap(summed, k, 0) if k else summed])
+
+    counts = tuple(len(blocks) for blocks in received)
+    half_shape = shape((len(counts) * GROUP_ROWS, block), BF16)
+    halves = pl.pallas_call(
+        functools.partial(sum_kernel, counts),
+        out_shape=[half_shape] * both,
+        in_specs=[VMEM] * sum(counts),
+        out_specs=[VMEM] * both,
+        compiler_params=PARAMS,
+        name="sums",
+    )(*[value for blocks in received for value in blocks])
+    if both == 2:
+        halves = [halves[0], swap(halves[1], 1, 0)]
     return pl.pallas_call(
-        functools.partial(finish_kernel, counts),
+        functools.partial(finish_kernel, both),
         out_shape=shape((rows, block), BF16),
-        in_specs=[VMEM] * (1 + sum(counts)),
+        in_specs=[VMEM] * (1 + both),
         out_specs=VMEM,
-        scratch_shapes=[pltpu.VMEM((store_count * GROUP_ROWS, block), BF16)],
         compiler_params=PARAMS,
         name="finish",
-    )(place, *[value for k in range(store_count) for value in received[k]])
+    )(place, *halves)
 
 
 def solution(mesh):

time: 76 us -> 54.8 us (0.72)
  starting transfers between devices: 35 us -> 23.5 us
  waiting for transfers between devices: 18.4 us -> 10.5 us
  Pallas kernels: 19.6 us -> 17.8 us
    ppermute x24 -> x17, starting transfers between devices: 35 us -> 23.5 us  [swap(): return lax.ppermute(value, ('store', 'tensor'), pairs)]
    ppermute x24 -> x17, waiting for transfers between devices: 18.4 us -> 10.5 us  [swap(): return lax.ppermute(value, ('store', 'tensor'), pairs)]
    pallas_call x2, Pallas kernels: 11.8 us -> 9.83 us  [shards(): pl.pallas_call(functools.partial(base_kernel, count), grid=(columns // st...]
    pallas_call x3 -> x4, Pallas kernels: 5.91 us -> 5.95 us  [the longest x2 4.87 us: shards(): pl.pallas_call(functools.partial(down_kernel, count, tensor_count, len(af...]
  transfers between devices with their start and end apart: 24 -> 17, of which waited for: 6 -> 6; matrix products, arithmetic and copies ran while one was open for 0% -> 0% of each run, Pallas kernels for 23% -> 28%
where the time goes in v2:
time: 54.8 us; the launch traced here: 54.5 us
  starting transfers between devices  23.5 us (43%)
  Pallas kernels  17.8 us (32%)
  waiting for transfers between devices  10.5 us (19%)
  local copies, waits for them, and re-layouts  2.58 us (5%)
    ppermute x17, starting transfers between devices, swap(): return lax.ppermute(value, ('store', 'tensor'), pairs)  23.5 us
    ppermute x17, waiting for transfers between devices, swap(): return lax.ppermute(value, ('store', 'tensor'), pairs)  10.5 us
    pallas_call x2, Pallas kernels, shards(): pl.pallas_call(functools.partial(base_kernel, count), grid=(columns // st...  9.83 us
    pallas_call x2, Pallas kernels, shards(): pl.pallas_call(functools.partial(down_kernel, count, tensor_count, len(af...  4.87 us
    unnamed x8, local copies, waits for them, and re-layouts  2.58 us
    pallas_call x1, Pallas kernels, shards(): pl.pallas_call(functools.partial(group_kernel, store_count), out_shape=[s...  1.26 us
  transfers between devices with their start and end apart: 17, of which 6 were waited for; matrix products, arithmetic and copies ran while one was open for 0% of the time, Pallas kernels for 28%

profile of v2, /device:TPU:0, one launch (start us, length us, event | category | flops | bytes accessed | tf_op | source)
XLA Modules:
  0.0 54.5 jit_solution(7196158770139687078)
XLA Ops:
  0.0 0.0 copy-start.1
  0.0 1.2 %copy-done.1 = bf16[256,2048]{1,0:T(8,128)(2,1)S(1)} copy-done((bf16[256,2048]{1,0:T(8,128)(2,1)S(1)}, bf16[256,2048]{1,0:T(8,128)(2,1)}, u32[]{:S(2)}) %copy-start.1) | copy-done | bytes 1048600
  1.2 0.0 copy-start.2
  1.2 0.7 %copy-done.2 = s32[256]{0:T(256)S(1)} copy-done((s32[256]{0:T(256)S(1)}, s32[256]{0:T(256)}, u32[]{:S(2)}) %copy-start.2) | copy-done | bytes 1048
  1.9 0.0 copy-start.3
  1.9 0.7 %copy-done.3 = s32[256]{0:T(256)S(1)} copy-done((s32[256]{0:T(256)S(1)}, s32[256]{0:T(256)}, u32[]{:S(2)}) %copy-start.3) | copy-done | bytes 1048
  2.6 1.3 %group_rows.1 = (bf16[256,256]{1,0:T(8,128)(2,1)S(1)}, bf16[64,2176]{1,0:T(8,128)(2,1)S(1)}, bf16[64,2176]{1,0:T(8,128)(2,1)S(1)}, bf16[64,2176]{1,0:T(8,128)(2,1)S(1)}, bf16[64,2176]{1,0:T(8,128)(2,1)S(1)}) custom-call(s32[1,256]{1,0:T(1,128)S(1)} %bitcast.5, s32[1,256]{1,0:T(1,128)S(1)} %bitcast.6, bf16[256,2048]{1,0:T(8,128)(2,1)S(1)} %copy-done.1), custom_call_target="tpu_custom_call" | custom-call | tf_op jit(solution)/shard_map/group_rows/pallas_call | solution.py:170
  3.8 0.5 collective-permute-start
  4.4 2.6 %collective-permute-start.7 = (bf16[64,2176]{1,0:T(8,128)(2,1)S(1)}, bf16[64,2176]{1,0:T(8,128)(2,1)S(1)}, u32[]{:S(2)}, u32[]{:S(2)}) collective-permute-start(bf16[64,2176]{1,0:T(8,128)(2,1)S(1)} %get-tuple-element.42), channel_id=1, source_target_pairs={{0,8},{1,9},{2,10},{3,11},{4,12},{5,13},{6,14},{7,15},{8,0},{9,1},... | collective-permute-start | bytes 835592 | tf_op jit(solution)/shard_map/ppermute | solution.py:168
  6.9 0.1 collective-permute-start.8
  7.0 0.0 collective-permute-done.refs_1_
  7.0 0.0 copy-start
  7.0 2.5 %low_products.2 = (f32[8,128]{1,0:T(8,128)S(1)}, f32[32,128]{1,0:T(8,128)S(1)}, f32[32,128]{1,0:T(8,128)S(1)}, f32[32,128]{1,0:T(8,128)S(1)}, f32[32,128]{1,0:T(8,128)S(1)}) custom-call(bf16[64,2176]{1,0:T(8,128)(2,1)S(1)} %get-tuple-element.31.refs_0_, bf16[64,2176]{1,0:T(8,128)(2,1)S(1)} %collective-permute-done.refs_1_, bf16[16,2048,128]{2,1,0:T(8,128)(2,1)} %refs_2_.7), custom_call_target="tpu_custom_call" | custom-call | flops 134217728 | bytes 2097152 | tf_op jit(solution)/shard_map/low_products/pallas_call | solution.py:201
  9.5 1.9 %collective-permute-start.1 = (f32[32,128]{1,0:T(8,128)S(1)}, f32[32,128]{1,0:T(8,128)S(1)}, u32[]{:S(2)}, u32[]{:S(2)}) collective-permute-start(f32[32,128]{1,0:T(8,128)S(1)} %get-tuple-element.35), channel_id=1, source_target_pairs={{0,1},{1,0},{2,3},{3,2},{4,5},{5,4},{6,7},{7,6},{8,9},{9,8},{10,11... | collective-permute-start | bytes 49160 | tf_op jit(solution)/shard_map/ppermute | solution.py:168
  11.4 2.6 %collective-permute-start.2 = (f32[32,128]{1,0:T(8,128)S(1)}, f32[32,128]{1,0:T(8,128)S(1)}, u32[]{:S(2)}, u32[]{:S(2)}) collective-permute-start(f32[32,128]{1,0:T(8,128)S(1)} %get-tuple-element.36), channel_id=1, source_target_pairs={{0,2},{1,3},{2,0},{3,1},{4,6},{5,7},{6,4},{7,5},{8,10},{9,11},{10,... | collective-permute-start | bytes 49160 | tf_op jit(solution)/shard_map/ppermute | solution.py:168
  14.0 0.0 collective-permute-start.3
  14.0 4.9 %base_products.2.base_ref = f32[128,2048]{1,0:T(8,128)S(1)} custom-call(bf16[64,2176]{1,0:T(8,128)(2,1)S(1)} %get-tuple-element.31.refs_0_, bf16[64,2176]{1,0:T(8,128)(2,1)S(1)} %collective-permute-done.refs_1_, bf16[2048,2048]{1,0:T(8,128)(2,1)} %refs_2_.6), custom_call_target="tpu_custom_call" | custom-call | flops 1073741824 | bytes 8388608 | tf_op jit(solution)/shard_map/base_products/pallas_call | solution.py:220
  18.9 0.0 collective-permute-done.1.refs_1_
  18.9 0.0 collective-permute-done.2.refs_2_
  18.9 0.6 %collective-permute-done.3.refs_3_ = f32[32,128]{1,0:T(8,128)S(1)} collective-permute-done((f32[32,128]{1,0:T(8,128)S(1)}, f32[32,128]{1,0:T(8,128)S(1)}, u32[]{:S(2)}, u32[]{:S(2)}) %collective-permute-start.3) | collective-permute-done | bytes 16416 | tf_op jit(solution)/shard_map/ppermute | solution.py:168
  19.5 0.0 copy-done
  19.5 0.4 up_products.2
  19.9 0.4 collective-permute-start.4
  20.3 3.5 %collective-permute-start.5 = (bf16[128,512]{1,0:T(8,128)(2,1)S(1)}, bf16[128,512]{1,0:T(8,128)(2,1)S(1)}, u32[]{:S(2)}, u32[]{:S(2)}) collective-permute-start(bf16[128,512]{1,0:T(8,128)(2,1)S(1)} %get-tuple-element.40), channel_id=1, source_target_pairs={{0,2},{1,3},{2,0},{3,1},{4,6},{5,7},{6,4},{7,5},{8,10},{9,11},{10,... | collective-permute-start | bytes 393224 | tf_op jit(solution)/shard_map/ppermute | solution.py:168
  23.8 0.0 collective-permute-done.7.refs_0_
  23.8 0.0 collective-permute-done.8.refs_1_
  23.8 2.4 %low_products.3 = (f32[8,128]{1,0:T(8,128)S(1)}, f32[32,128]{1,0:T(8,128)S(1)}, f32[32,128]{1,0:T(8,128)S(1)}, f32[32,128]{1,0:T(8,128)S(1)}, f32[32,128]{1,0:T(8,128)S(1)}) custom-call(bf16[64,2176]{1,0:T(8,128)(2,1)S(1)} %collective-permute-done.7.refs_0_, bf16[64,2176]{1,0:T(8,128)(2,1)S(1)} %collective-permute-done.8.refs_1_, ...), custom_call_target="tpu_custom_call" | custom-call | flops 134217728 | bytes 2097152 | tf_op jit(solution)/shard_map/low_products/pallas_call | solution.py:201
  26.2 0.1 collective-permute-start.9
  26.3 1.0 %collective-permute-start.10 = (f32[32,128]{1,0:T(8,128)S(1)}, f32[32,128]{1,0:T(8,128)S(1)}, u32[]{:S(2)}, u32[]{:S(2)}) collective-permute-start(f32[32,128]{1,0:T(8,128)S(1)} %get-tuple-element.47), channel_id=1, source_target_pairs={{0,2},{1,3},{2,0},{3,1},{4,6},{5,7},{6,4},{7,5},{8,10},{9,11},{10,... | collective-permute-start | bytes 49160 | tf_op jit(solution)/shard_map/ppermute | solution.py:168
  27.4 3.3 %collective-permute-start.11 = (f32[32,128]{1,0:T(8,128)S(1)}, f32[32,128]{1,0:T(8,128)S(1)}, u32[]{:S(2)}, u32[]{:S(2)}) collective-permute-start(f32[32,128]{1,0:T(8,128)S(1)} %get-tuple-element.48), channel_id=1, source_target_pairs={{0,3},{1,2},{2,1},{3,0},{4,7},{5,6},{6,5},{7,4},{8,11},{9,10},{10,... | collective-permute-start | bytes 49160 | tf_op jit(solution)/shard_map/ppermute | solution.py:168
  30.6 4.9 %base_products.3.base_ref = f32[128,2048]{1,0:T(8,128)S(1)} custom-call(bf16[64,2176]{1,0:T(8,128)(2,1)S(1)} %collective-permute-done.7.refs_0_, bf16[64,2176]{1,0:T(8,128)(2,1)S(1)} %collective-permute-done.8.refs_1_, bf16[2048,2048]{1,0:T(8,128)(2,1)} %refs_2_.6), custom_call_target="tpu_custom_call" | custom-call | flops 1073741824 | bytes 8388608 | tf_op jit(solution)/shard_map/base_products/pallas_call | solution.py:220
  35.6 0.0 collective-permute-done.9.refs_1_
  35.6 0.6 %collective-permute-start.6 = (bf16[128,512]{1,0:T(8,128)(2,1)S(1)}, bf16[128,512]{1,0:T(8,128)(2,1)S(1)}, u32[]{:S(2)}, u32[]{:S(2)}) collective-permute-start(bf16[128,512]{1,0:T(8,128)(2,1)S(1)} %get-tuple-element.41), channel_id=1, source_target_pairs={{0,3},{1,2},{2,1},{3,0},{4,7},{5,6},{6,5},{7,4},{8,11},{9,10},{10,... | collective-permute-start | bytes 393224 | tf_op jit(solution)/shard_map/ppermute | solution.py:168
  36.2 0.0 collective-permute-done.10.refs_2_
  36.2 0.0 collective-permute-done.11.refs_3_
  36.2 0.4 up_products.3
  36.6 1.6 %collective-permute-start.12 = (bf16[128,512]{1,0:T(8,128)(2,1)S(1)}, bf16[128,512]{1,0:T(8,128)(2,1)S(1)}, u32[]{:S(2)}, u32[]{:S(2)}) collective-permute-start(bf16[128,512]{1,0:T(8,128)(2,1)S(1)} %get-tuple-element.49), channel_id=1, source_target_pairs={{0,8},{1,9},{2,10},{3,11},{4,12},{5,13},{6,14},{7,15},{8,0},{9,1},... | collective-permute-start | bytes 393224 | tf_op jit(solution)/shard_map/ppermute | solution.py:168
  38.2 0.0 collective-permute-start.13
  38.2 0.0 collective-permute-done.4.refs_1_
  38.2 4.7 %collective-permute-start.14 = (bf16[128,512]{1,0:T(8,128)(2,1)S(1)}, bf16[128,512]{1,0:T(8,128)(2,1)S(1)}, u32[]{:S(2)}, u32[]{:S(2)}) collective-permute-start(bf16[128,512]{1,0:T(8,128)(2,1)S(1)} %get-tuple-element.51), channel_id=1, source_target_pairs={{0,10},{1,11},{2,8},{3,9},{4,14},{5,15},{6,12},{7,13},{8,2},{9,3},... | collective-permute-start | bytes 393224 | tf_op jit(solution)/shard_map/ppermute | solution.py:168
  42.9 0.0 collective-permute-done.5.refs_2_
  42.9 0.5 collective-permute-start.15
  43.4 0.2 collective-permute-done.6.refs_3_
  43.6 0.4 collective-permute-done.12.refs_4_
  44.0 4.1 %collective-permute-done.13.refs_5_ = bf16[128,512]{1,0:T(8,128)(2,1)S(1)} collective-permute-done((bf16[128,512]{1,0:T(8,128)(2,1)S(1)}, bf16[128,512]{1,0:T(8,128)(2,1)S(1)}, u32[]{:S(2)}, u32[]{:S(2)}) %collective-permute-start.13) | collective-permute-done | bytes 131104 | tf_op jit(solution)/shard_map/ppermute | solution.py:168
  48.1 3.9 %collective-permute-done.14.refs_6_ = bf16[128,512]{1,0:T(8,128)(2,1)S(1)} collective-permute-done((bf16[128,512]{1,0:T(8,128)(2,1)S(1)}, bf16[128,512]{1,0:T(8,128)(2,1)S(1)}, u32[]{:S(2)}, u32[]{:S(2)}) %collective-permute-start.14) | collective-permute-done | bytes 131104 | tf_op jit(solution)/shard_map/ppermute | solution.py:168
  51.9 0.0 collective-permute-done.15.refs_7_
  51.9 0.1 sums.1
  52.1 0.1 collective-permute-start.16
  52.2 1.3 %collective-permute-done.16.refs_1_ = bf16[128,512]{1,0:T(8,128)(2,1)S(1)} collective-permute-done((bf16[128,512]{1,0:T(8,128)(2,1)S(1)}, bf16[128,512]{1,0:T(8,128)(2,1)S(1)}, u32[]{:S(2)}, u32[]{:S(2)}) %collective-permute-start.16) | collective-permute-done | bytes 131104 | tf_op jit(solution)/shard_map/ppermute | solution.py:168
  53.5 1.0 %finish.1 = bf16[256,512]{1,0:T(8,128)(2,1)} custom-call(bf16[256,256]{1,0:T(8,128)(2,1)S(1)} %get-tuple-element.30.place_ref, bf16[128,512]{1,0:T(8,128)(2,1)S(1)} %get-tuple-element.53.refs_0_, bf16[128,512]{1,0:T(8,128)(2,1)S(1)} %collective-permute-done.16.refs_1_), custom_call_target="tpu_custom_call" | custom-call | tf_op jit(solution)/shard_map/finish/pallas_call | solution.py:266
Async XLA Ops:
  0.0 1.2 %copy-start.1 = (bf16[256,2048]{1,0:T(8,128)(2,1)S(1)}, bf16[256,2048]{1,0:T(8,128)(2,1)}, u32[]{:S(2)}) copy-start(bf16[256,2048]{1,0:T(8,128)(2,1)} %tokens_hbm.1) | copy-start | bytes 3145732
  1.2 0.7 %copy-start.2 = (s32[256]{0:T(256)S(1)}, s32[256]{0:T(256)}, u32[]{:S(2)}) copy-start(s32[256]{0:T(256)} %param.10) | copy-start | bytes 3076
  1.9 0.7 %copy-start.3 = (s32[256]{0:T(256)S(1)}, s32[256]{0:T(256)}, u32[]{:S(2)}) copy-start(s32[256]{0:T(256)} %param.11) | copy-start | bytes 3076
  3.8 3.2 %collective-permute-start = (bf16[64,2176]{1,0:T(8,128)(2,1)S(1)}, bf16[64,2176]{1,0:T(8,128)(2,1)S(1)}, u32[]{:S(2)}, u32[]{:S(2)}) collective-permute-start(bf16[64,2176]{1,0:T(8,128)(2,1)S(1)} %get-tuple-element.32), channel_id=1, source_target_pairs={{0,4},{1,5},{2,6},{3,7},{4,0},{5,1},{6,2},{7,3},{8,12},{9,13},{10,... | collective-permute-start | bytes 835592 | tf_op jit(solution)/shard_map/ppermute | solution.py:168
  4.4 19.4 %collective-permute-start.7 = (bf16[64,2176]{1,0:T(8,128)(2,1)S(1)}, bf16[64,2176]{1,0:T(8,128)(2,1)S(1)}, u32[]{:S(2)}, u32[]{:S(2)}) collective-permute-start(bf16[64,2176]{1,0:T(8,128)(2,1)S(1)} %get-tuple-element.42), channel_id=1, source_target_pairs={{0,8},{1,9},{2,10},{3,11},{4,12},{5,13},{6,14},{7,15},{8,0},{9,1},... | collective-permute-start | bytes 835592 | tf_op jit(solution)/shard_map/ppermute | solution.py:168
  6.9 16.8 %collective-permute-start.8 = (bf16[64,2176]{1,0:T(8,128)(2,1)S(1)}, bf16[64,2176]{1,0:T(8,128)(2,1)S(1)}, u32[]{:S(2)}, u32[]{:S(2)}) collective-permute-start(bf16[64,2176]{1,0:T(8,128)(2,1)S(1)} %get-tuple-element.43), channel_id=1, source_target_pairs={{0,12},{1,13},{2,14},{3,15},{4,8},{5,9},{6,10},{7,11},{8,4},{9,5},... | collective-permute-start | bytes 835592 | tf_op jit(solution)/shard_map/ppermute | solution.py:168
  7.0 12.5 %copy-start = (bf16[16,16,2048]{2,1,0:T(8,128)(2,1)S(1)}, bf16[16,16,2048]{2,1,0:T(8,128)(2,1)}, u32[]{:S(2)}) copy-start(bf16[16,16,2048]{2,1,0:T(8,128)(2,1)} %param.9) | copy-start | bytes 3145732
  9.5 9.4 %collective-permute-start.1 = (f32[32,128]{1,0:T(8,128)S(1)}, f32[32,128]{1,0:T(8,128)S(1)}, u32[]{:S(2)}, u32[]{:S(2)}) collective-permute-start(f32[32,128]{1,0:T(8,128)S(1)} %get-tuple-element.35), channel_id=1, source_target_pairs={{0,1},{1,0},{2,3},{3,2},{4,5},{5,4},{6,7},{7,6},{8,9},{9,8},{10,11... | collective-permute-start | bytes 49160 | tf_op jit(solution)/shard_map/ppermute | solution.py:168
  11.4 7.5 %collective-permute-start.2 = (f32[32,128]{1,0:T(8,128)S(1)}, f32[32,128]{1,0:T(8,128)S(1)}, u32[]{:S(2)}, u32[]{:S(2)}) collective-permute-start(f32[32,128]{1,0:T(8,128)S(1)} %get-tuple-element.36), channel_id=1, source_target_pairs={{0,2},{1,3},{2,0},{3,1},{4,6},{5,7},{6,4},{7,5},{8,10},{9,11},{10,... | collective-permute-start | bytes 49160 | tf_op jit(solution)/shard_map/ppermute | solution.py:168
  14.0 5.5 %collective-permute-start.3 = (f32[32,128]{1,0:T(8,128)S(1)}, f32[32,128]{1,0:T(8,128)S(1)}, u32[]{:S(2)}, u32[]{:S(2)}) collective-permute-start(f32[32,128]{1,0:T(8,128)S(1)} %get-tuple-element.37), channel_id=1, source_target_pairs={{0,3},{1,2},{2,1},{3,0},{4,7},{5,6},{6,5},{7,4},{8,11},{9,10},{10,... | collective-permute-start | bytes 49160 | tf_op jit(solution)/shard_map/ppermute | solution.py:168
  19.9 18.3 %collective-permute-start.4 = (bf16[128,512]{1,0:T(8,128)(2,1)S(1)}, bf16[128,512]{1,0:T(8,128)(2,1)S(1)}, u32[]{:S(2)}, u32[]{:S(2)}) collective-permute-start(bf16[128,512]{1,0:T(8,128)(2,1)S(1)} %get-tuple-element.39), channel_id=1, source_target_pairs={{0,1},{1,0},{2,3},{3,2},{4,5},{5,4},{6,7},{7,6},{8,9},{9,8},{10,11... | collective-permute-start | bytes 393224 | tf_op jit(solution)/shard_map/ppermute | solution.py:168
  20.3 22.6 %collective-permute-start.5 = (bf16[128,512]{1,0:T(8,128)(2,1)S(1)}, bf16[128,512]{1,0:T(8,128)(2,1)S(1)}, u32[]{:S(2)}, u32[]{:S(2)}) collective-permute-start(bf16[128,512]{1,0:T(8,128)(2,1)S(1)} %get-tuple-element.40), channel_id=1, source_target_pairs={{0,2},{1,3},{2,0},{3,1},{4,6},{5,7},{6,4},{7,5},{8,10},{9,11},{10,... | collective-permute-start | bytes 393224 | tf_op jit(solution)/shard_map/ppermute | solution.py:168
  26.2 9.4 %collective-permute-start.9 = (f32[32,128]{1,0:T(8,128)S(1)}, f32[32,128]{1,0:T(8,128)S(1)}, u32[]{:S(2)}, u32[]{:S(2)}) collective-permute-start(f32[32,128]{1,0:T(8,128)S(1)} %get-tuple-element.46), channel_id=1, source_target_pairs={{0,1},{1,0},{2,3},{3,2},{4,5},{5,4},{6,7},{7,6},{8,9},{9,8},{10,11... | collective-permute-start | bytes 49160 | tf_op jit(solution)/shard_map/ppermute | solution.py:168
  26.3 9.9 %collective-permute-start.10 = (f32[32,128]{1,0:T(8,128)S(1)}, f32[32,128]{1,0:T(8,128)S(1)}, u32[]{:S(2)}, u32[]{:S(2)}) collective-permute-start(f32[32,128]{1,0:T(8,128)S(1)} %get-tuple-element.47), channel_id=1, source_target_pairs={{0,2},{1,3},{2,0},{3,1},{4,6},{5,7},{6,4},{7,5},{8,10},{9,11},{10,... | collective-permute-start | bytes 49160 | tf_op jit(solution)/shard_map/ppermute | solution.py:168
  27.4 8.8 %collective-permute-start.11 = (f32[32,128]{1,0:T(8,128)S(1)}, f32[32,128]{1,0:T(8,128)S(1)}, u32[]{:S(2)}, u32[]{:S(2)}) collective-permute-start(f32[32,128]{1,0:T(8,128)S(1)} %get-tuple-element.48), channel_id=1, source_target_pairs={{0,3},{1,2},{2,1},{3,0},{4,7},{5,6},{6,5},{7,4},{8,11},{9,10},{10,... | collective-permute-start | bytes 49160 | tf_op jit(solution)/shard_map/ppermute | solution.py:168
  35.6 8.0 %collective-permute-start.6 = (bf16[128,512]{1,0:T(8,128)(2,1)S(1)}, bf16[128,512]{1,0:T(8,128)(2,1)S(1)}, u32[]{:S(2)}, u32[]{:S(2)}) collective-permute-start(bf16[128,512]{1,0:T(8,128)(2,1)S(1)} %get-tuple-element.41), channel_id=1, source_target_pairs={{0,3},{1,2},{2,1},{3,0},{4,7},{5,6},{6,5},{7,4},{8,11},{9,10},{10,... | collective-permute-start | bytes 393224 | tf_op jit(solution)/shard_map/ppermute | solution.py:168
  36.6 7.4 %collective-permute-start.12 = (bf16[128,512]{1,0:T(8,128)(2,1)S(1)}, bf16[128,512]{1,0:T(8,128)(2,1)S(1)}, u32[]{:S(2)}, u32[]{:S(2)}) collective-permute-start(bf16[128,512]{1,0:T(8,128)(2,1)S(1)} %get-tuple-element.49), channel_id=1, source_target_pairs={{0,8},{1,9},{2,10},{3,11},{4,12},{5,13},{6,14},{7,15},{8,0},{9,1},... | collective-permute-start | bytes 393224 | tf_op jit(solution)/shard_map/ppermute | solution.py:168
  38.2 9.9 %collective-permute-start.13 = (bf16[128,512]{1,0:T(8,128)(2,1)S(1)}, bf16[128,512]{1,0:T(8,128)(2,1)S(1)}, u32[]{:S(2)}, u32[]{:S(2)}) collective-permute-start(bf16[128,512]{1,0:T(8,128)(2,1)S(1)} %get-tuple-element.50), channel_id=1, source_target_pairs={{0,9},{1,8},{2,11},{3,10},{4,13},{5,12},{6,15},{7,14},{8,1},{9,0},... | collective-permute-start | bytes 393224 | tf_op jit(solution)/shard_map/ppermute | solution.py:168
  38.2 13.8 %collective-permute-start.14 = (bf16[128,512]{1,0:T(8,128)(2,1)S(1)}, bf16[128,512]{1,0:T(8,128)(2,1)S(1)}, u32[]{:S(2)}, u32[]{:S(2)}) collective-permute-start(bf16[128,512]{1,0:T(8,128)(2,1)S(1)} %get-tuple-element.51), channel_id=1, source_target_pairs={{0,10},{1,11},{2,8},{3,9},{4,14},{5,15},{6,12},{7,13},{8,2},{9,3},... | collective-permute-start | bytes 393224 | tf_op jit(solution)/shard_map/ppermute | solution.py:168
  42.9 9.1 %collective-permute-start.15 = (bf16[128,512]{1,0:T(8,128)(2,1)S(1)}, bf16[128,512]{1,0:T(8,128)(2,1)S(1)}, u32[]{:S(2)}, u32[]{:S(2)}) collective-permute-start(bf16[128,512]{1,0:T(8,128)(2,1)S(1)} %get-tuple-element.52), channel_id=1, source_target_pairs={{0,11},{1,10},{2,9},{3,8},{4,15},{5,14},{6,13},{7,12},{8,3},{9,2},... | collective-permute-start | bytes 393224 | tf_op jit(solution)/shard_map/ppermute | solution.py:168
  52.1 1.4 %collective-permute-start.16 = (bf16[128,512]{1,0:T(8,128)(2,1)S(1)}, bf16[128,512]{1,0:T(8,128)(2,1)S(1)}, u32[]{:S(2)}, u32[]{:S(2)}) collective-permute-start(bf16[128,512]{1,0:T(8,128)(2,1)S(1)} %get-tuple-element.54), channel_id=1, source_target_pairs={{0,4},{1,5},{2,6},{3,7},{4,0},{5,1},{6,2},{7,3},{8,12},{9,13},{10,... | collective-permute-start | bytes 393224 | tf_op jit(solution)/shard_map/ppermute | solution.py:168

commit v3 on v2

v3 whole, which is shorter than its diff:
```python
import functools

import jax
import jax.numpy as jnp
from jax import lax
from jax.experimental import pallas as pl
from jax.experimental.pallas import tpu as pltpu
from jax.sharding import PartitionSpec as P

SLOTS = 2
GROUP_ROWS = 64
LANES = 128
F32 = jnp.float32
BF16 = jnp.bfloat16
VMEM = pl.BlockSpec(memory_space=pltpu.VMEM)
ANY = pl.BlockSpec(memory_space=pl.ANY)
PARAMS = pltpu.CompilerParams(vmem_limit_bytes=16 * 1024 * 1024)
WIDE = pltpu.CompilerParams(vmem_limit_bytes=48 * 1024 * 1024)
TWO_STEP_LOW = (False, False)
TWO_STEP_SHARES = (False, False)


def contract(a, b, dim_a, dim_b):
    return lax.dot_general(a, b, (((dim_a,), (dim_b,)), ((), ())), preferred_element_type=F32)


def group_kernel(store_count, adapters, codes_ref, tokens_ref, *outs):
    place_ref, group_refs = outs[0], outs[1:]
    me = lax.axis_index("store")
    rows, width = tokens_ref.shape
    codes = codes_ref[...]
    owner = codes // (SLOTS * adapters)
    relative = owner ^ me
    padded = max(8, store_count)
    mine = lax.broadcasted_iota(jnp.int32, (padded, rows), 0) == relative
    upto = lax.broadcasted_iota(jnp.int32, (rows, rows), 0) <= lax.broadcasted_iota(jnp.int32, (rows, rows), 1)
    count = contract(mine.astype(F32).astype(BF16), upto.astype(F32).astype(BF16), 1, 0)
    rank = jnp.sum(jnp.where(mine, count, 0.0), axis=0, keepdims=True).astype(jnp.int32) - 1
    tags = jnp.broadcast_to((codes % adapters + 1).astype(F32), (LANES, rows)).astype(BF16)
    position = lax.broadcasted_iota(jnp.int32, (GROUP_ROWS, rows), 0)
    places = []
    for k in range(store_count):
        place = ((relative == k) & (rank == position)).astype(F32).astype(BF16)
        place_ref[k * GROUP_ROWS : (k + 1) * GROUP_ROWS, :] = place
        places.append(place)
    for place, out in zip(places, group_refs):
        out[:, :width] = contract(place, tokens_ref[...], 1, 0).astype(BF16)
        out[:, width:] = contract(place, tags, 1, 1).astype(BF16)


def down_kernel(group_count, tensor_count, after_count, piece_count, *refs):
    xs, down_ref, refs = refs[:group_count], refs[group_count], refs[group_count + 1 + after_count :]
    tags_ref, pieces = refs[0], refs[1 : 1 + piece_count]
    low, low_t, *fetch = refs[1 + piece_count :]
    me = lax.axis_index("tensor")
    adapters, width, ranks = down_ref.shape
    chosen, copies = [], []
    for g, x in enumerate(xs):
        tag = x[:, width:].astype(F32)
        top = jnp.max(tag)
        bottom = jnp.min(jnp.where(tag > 0, tag, top))
        indices = [jnp.clip(value.astype(jnp.int32) - 1, 0, adapters - 1) for value in (bottom, top)]
        chosen.append((tag, top, indices))
        if fetch:
            for slot, index in enumerate(indices):
                copy = pltpu.make_async_copy(down_ref.at[index], fetch[0].at[g, slot], fetch[1].at[g, slot])
                copy.start()
                copies.append(copy)
    for g, x in enumerate(xs):
        tag, top, indices = chosen[g]
        if fetch:
            copies[2 * g].wait()
            copies[2 * g + 1].wait()
            maps = [fetch[0][g, slot] for slot in range(2)]
        else:
            maps = [down_ref[index] for index in indices]
        first, second = (contract(x[:, :width], value, 1, 0) for value in maps)
        low[g * GROUP_ROWS : (g + 1) * GROUP_ROWS, :ranks] = jnp.where(tag == top, second, first)
        low[g * GROUP_ROWS : (g + 1) * GROUP_ROWS, ranks:] = tag
    low_t[...] = low[:, :ranks].T
    tags_ref[...] = low[:, ranks:].T[:8]
    portion = ranks // 2 // tensor_count
    for j in range(tensor_count):
        out, place = pieces[j % piece_count], j // piece_count * 2 * portion
        to = me ^ j
        for half in range(2):
            value = jnp.zeros((portion, low_t.shape[1]), F32)
            for b in range(tensor_count):
                start = half * (ranks // 2) + b * portion
                value = jnp.where(to == b, low_t[start : start + portion, :], value)
            out[place + half * portion : place + (half + 1) * portion, :] = value


def fold_kernel(size, mine_ref, got_ref, keep_ref, send_ref):
    for i in range(mine_ref.shape[0] // size):
        out, rows = (keep_ref, send_ref)[i % 2], pl.ds(i * size, size)
        total = mine_ref[rows, :].astype(F32) + got_ref[rows, :].astype(F32)
        out[i // 2 * size : (i // 2 + 1) * size, :] = total.astype(out.dtype)


def fold(size, mine, got, keep_type):
    rows, columns = mine.shape
    return pl.pallas_call(
        functools.partial(fold_kernel, size),
        out_shape=[
            jax.ShapeDtypeStruct((rows // 2, columns), keep_type),
            jax.ShapeDtypeStruct((rows // 2, columns), got.dtype),
        ],
        in_specs=[VMEM] * 2,
        out_specs=[VMEM] * 2,
        compiler_params=PARAMS,
        name="fold",
    )(mine, got)


def base_kernel(group_count, *refs):
    xs, weight_ref, out_ref = refs[:group_count], refs[group_count], refs[group_count + 1]
    width = weight_ref.shape[0]
    x = jnp.concatenate([x[:, :width] for x in xs], axis=0)
    step = 512
    for i in range(out_ref.shape[1] // step):
        out_ref[:, i * step : (i + 1) * step] = contract(x, weight_ref[:, i * step : (i + 1) * step], 1, 0)


def up_kernel(tensor_count, adapters, piece_count, out_count, base_ref, tags_ref, up_ref, *refs):
    pieces, outs, mixed = refs[:piece_count], refs[piece_count:-1], refs[-1]
    me = lax.axis_index("tensor")
    low = pieces[0][...]
    for value in pieces[1:]:
        low = low + value[...]
    low = low.astype(BF16).astype(F32)
    portion = low.shape[0] // 2
    tag = tags_ref[0:1, :]
    for half in range(2):
        part = low[half * portion : (half + 1) * portion, :]
        for a in range(adapters):
            mixed[half, a * portion : (a + 1) * portion, :] = jnp.where(tag == a + 1, part, 0.0)
    block = up_ref.shape[1] // tensor_count
    for j in range(tensor_count):
        to = me ^ j
        columns = pl.ds(pl.multiple_of(to * block, block), block)
        total = base_ref[:, columns] + contract(
            mixed[to // (tensor_count // 2)].astype(BF16), up_ref[:, columns], 0, 0
        )
        rows = outs[0].shape[0] * out_count // tensor_count
        for p in range(len(outs) // out_count):
            out, place = outs[p * out_count + j % out_count], j // out_count * rows
            out[place : place + rows, :] = total[p * rows : (p + 1) * rows, :].astype(out.dtype)


def sum_kernel(counts, *refs):
    outs, first = refs[sum(counts) :], 0
    for p, count in enumerate(counts):
        for h, out in enumerate(outs):
            rows = pl.ds(h * GROUP_ROWS, GROUP_ROWS)
            total = refs[first][rows, :].astype(F32)
            for ref in refs[first + 1 : first + count]:
                total = total + ref[rows, :].astype(F32)
            out[p * GROUP_ROWS : (p + 1) * GROUP_ROWS, :] = total.astype(BF16)
        first += count


def finish_kernel(both, place_ref, *refs):
    halves, out_ref = refs[:both], refs[both]
    groups = []
    for k in range(place_ref.shape[0] // GROUP_ROWS):
        p = k // both
        groups.append(halves[k % both][p * GROUP_ROWS : (p + 1) * GROUP_ROWS, :])
    out_ref[...] = contract(place_ref[...], jnp.concatenate(groups, axis=0), 0, 0).astype(BF16)


def shards(tokens, weight, down_maps, up_maps, local_ids, slot_index):
    store_count, tensor_count = lax.axis_size("store"), lax.axis_size("tensor")
    rows, width = tokens.shape
    adapters, _, ranks = down_maps.shape
    columns = weight.shape[1]
    portion = up_maps.shape[1]
    block = columns // tensor_count
    up_flat = up_maps.reshape(adapters * portion, columns)
    shape = jax.ShapeDtypeStruct

    def swap(value, k, j):
        pairs = [
            (s * tensor_count + t, (s ^ k) * tensor_count + (t ^ j))
            for s in range(store_count)
            for t in range(tensor_count)
        ]
        return lax.ppermute(value, ("store", "tensor"), pairs)

    place, *groups = pl.pallas_call(
        functools.partial(group_kernel, store_count, adapters),
        out_shape=[shape((store_count * GROUP_ROWS, rows), BF16)]
        + [shape((GROUP_ROWS, width + LANES), BF16)] * store_count,
        in_specs=[VMEM] * 2,
        out_specs=[VMEM] * (store_count + 1),
        compiler_params=PARAMS,
        name="group_rows",
    )((slot_index * adapters + local_ids).reshape(1, rows), tokens)

    both = min(2, store_count)
    far = range(2, store_count)
    near = range(both)
    arrived = {}
    for k in (*near, *far):
        arrived[k] = swap(groups[k], k, 0) if k else groups[k]

    received, after = [], []
    for part in (near, far):
        part = list(part)
        if not part:
            continue
        count = len(part)
        part_rows = count * GROUP_ROWS
        xs = [arrived[k] for k in part]
        piece = 2 * portion
        two_step = tensor_count > 4 or TWO_STEP_LOW[bool(after)]
        piece_count = 2 if two_step else tensor_count
        tags, *pieces = pl.pallas_call(
            functools.partial(down_kernel, count, tensor_count, len(after), piece_count),
            out_shape=[shape((8, part_rows), F32)] + [shape((tensor_count // piece_count * piece, part_rows), F32)] * piece_count,
            in_specs=[VMEM] * count + [VMEM if after else ANY] + [ANY] * len(after),
            out_specs=[VMEM] * (1 + piece_count),
            scratch_shapes=[
                pltpu.VMEM((part_rows, 2 * ranks), F32),
                pltpu.VMEM((ranks, part_rows), F32),
            ]
            + ([] if after else [pltpu.VMEM((count, 2, width, ranks), BF16), pltpu.SemaphoreType.DMA((count, 2))]),
            compiler_params=PARAMS if after else WIDE,
            cost_estimate=pl.CostEstimate(
                flops=4 * part_rows * width * ranks, bytes_accessed=count * 4 * width * ranks, transcendentals=0
            ),
            name="low_products",
        )(*xs, down_maps, *after)
        if two_step:
            keep, send = pieces
            distance, got = 1, swap(send, 0, 1)
            while 2 * distance < tensor_count:
                distance *= 2
                keep, send = fold(piece, keep, got, F32)
                got = swap(send, 0, distance)
            pieces = [keep, got]
        else:
            pieces = [swap(value, 0, j) if j else value for j, value in enumerate(pieces)]
        base = pl.pallas_call(
            functools.partial(base_kernel, count),
            out_shape=shape((part_rows, columns), F32),
            in_specs=[VMEM] * (count + 1),
            out_specs=VMEM,
            compiler_params=PARAMS,
            cost_estimate=pl.CostEstimate(
                flops=2 * part_rows * width * columns, bytes_accessed=2 * width * columns, transcendentals=0
            ),
            name="base_products",
        )(*xs, weight)
        direct = store_count * tensor_count > 16 or not TWO_STEP_SHARES[bool(after)]
        out_count = tensor_count if direct else 2
        pair_rows = both * GROUP_ROWS
        shares = pl.pallas_call(
            functools.partial(up_kernel, tensor_count, adapters, len(pieces), out_count),
            out_shape=[
                shape((tensor_count // out_count * pair_rows, block), BF16 if direct or i % 2 else F32)
                for i in range(count // both * out_count)
            ],
            in_specs=[VMEM] * (3 + len(pieces)),
            out_specs=[VMEM] * (count // both * out_count),
            scratch_shapes=[pltpu.VMEM((2, adapters * portion, part_rows), F32)],
            compiler_params=PARAMS,
            name="up_products",
        )(base, tags, up_flat, *pieces)
        after = shares[-1:]
        for p in range(count // both):
            k = part[p * both]
            mine = shares[p * out_count : (p + 1) * out_count]
            if not direct:
                keep, send = mine
                distance, got = 1, swap(send, 0, 1)
                while 2 * distance < tensor_count:
                    distance *= 2
                    last = 2 * distance == tensor_count
                    keep, send = fold(pair_rows, keep, got, BF16 if k and last else F32)
                    got = swap(send, k if last else 0, distance)
                received.append([swap(keep, k, 0) if k else keep, got])
            elif store_count * tensor_count <= 16:
                blocks = [swap(mine[j], k, j) if k or j else mine[j] for j in reversed(range(tensor_count))]
                received.append(blocks[::-1])
            else:
                order = jnp.arange(tensor_count, dtype=jnp.int32) ^ lax.axis_index("tensor")
                stacked = jnp.take(jnp.stack(mine), order, axis=0)
                summed = lax.all_to_all(stacked, "tensor", 0, 0, tiled=True).astype(F32).sum(0).astype(BF16)
                received.append([swap(summed, k, 0) if k else summed])

    counts = tuple(len(blocks) for blocks in received)
    half_shape = shape((len(counts) * GROUP_ROWS, block), BF16)
    halves = pl.pallas_call(
        functools.partial(sum_kernel, counts),
        out_shape=[half_shape] * both,
        in_specs=[VMEM] * sum(counts),
        out_specs=[VMEM] * both,
        compiler_params=PARAMS,
        name="sums",
    )(*[value for blocks in received for value in blocks])
    if both == 2:
        halves = [halves[0], swap(halves[1], 1, 0)]
    return pl.pallas_call(
        functools.partial(finish_kernel, both),
        out_shape=shape((rows, block), BF16),
        in_specs=[VMEM] * (1 + both),
        out_specs=VMEM,
        compiler_params=PARAMS,
        name="finish",
    )(place, *halves)


def solution(mesh):
    in_specs = (
        P(("groups", "store"), "tensor"),
        P("tensor", None),
        P(("groups", "store"), "tensor", None),
        P(("groups", "store"), "tensor", None),
        P(("groups", "store")),
        P(("groups", "store")),
    )
    out_specs = P(("groups", "store"), "tensor")
    return jax.shard_map(shards, mesh=mesh, in_specs=in_specs, out_specs=out_specs, check_vma=False)
```

time: 54.8 us -> 48 us (0.88)
  Pallas kernels: 17.8 us -> 8.52 us
  waiting for transfers between devices: 10.5 us -> 13.5 us
  local copies, waits for them, and re-layouts: 2.58 us -> 1.36 us
  other arithmetic: 0 us -> 0.85 us
    pallas_call x5, Pallas kernels: 11.8 us -> 4.4 us  [the longest x2 2.53 us: shards(): pl.pallas_call(functools.partial(base_kernel, count), out_shape=shape((pa...]
    ppermute x17, waiting for transfers between devices: 10.5 us -> 13.5 us  [swap(): return lax.ppermute(value, ('store', 'tensor'), pairs)]
    pallas_call x2, Pallas kernels: 4.87 us -> 3.04 us  [shards(): pl.pallas_call(functools.partial(down_kernel, count, tensor_count, len(af...]
    unnamed x8, local copies, waits for them, and re-layouts: 2.58 us -> 1.36 us
    add x0 -> x1, other arithmetic: none -> 0.85 us  [shards(): slot_index * adapters + local_ids]
  transfers between devices with their start and end apart: 17 -> 17, of which waited for: 6 -> 6; matrix products, arithmetic and copies ran while one was open for 0% -> 0% of each run, Pallas kernels for 28% -> 13%
where the time goes in v3:
time: 48 us; the launch traced here: 47.8 us
  starting transfers between devices  23.5 us (49%)
  waiting for transfers between devices  13.5 us (28%)
  Pallas kernels  8.52 us (18%)
  local copies, waits for them, and re-layouts  1.36 us (3%)
  other arithmetic  0.85 us (2%)
    ppermute x17, starting transfers between devices, swap(): return lax.ppermute(value, ('store', 'tensor'), pairs)  23.5 us
    ppermute x17, waiting for transfers between devices, swap(): return lax.ppermute(value, ('store', 'tensor'), pairs)  13.5 us
    pallas_call x2, Pallas kernels, shards(): pl.pallas_call(functools.partial(down_kernel, count, tensor_count, len(af...  3.04 us
    pallas_call x2, Pallas kernels, shards(): pl.pallas_call(functools.partial(base_kernel, count), out_shape=shape((pa...  2.53 us
    unnamed x8, local copies, waits for them, and re-layouts  1.36 us
    pallas_call x1, Pallas kernels, shards(): pl.pallas_call(functools.partial(group_kernel, store_count, adapters), ou...  1.12 us
  transfers between devices with their start and end apart: 17, of which 6 were waited for; matrix products, arithmetic and copies ran while one was open for 0% of the time, Pallas kernels for 13%

profile of v3, /device:TPU:0, one launch (start us, length us, event | category | flops | bytes accessed | tf_op | source)
XLA Modules:
  0.0 47.8 jit_solution(4542647525208391165)
XLA Ops:
  0.0 0.0 copy-start
  0.0 0.8 %multiply_add_fusion = s32[256]{0:T(256)S(1)} fusion(s32[256]{0:T(256)} %param.10, s32[256]{0:T(256)} %param.11), kind=kLoop, calls=%fused_computation | loop fusion | flops 512 | bytes 3072 | tf_op jit(solution)/shard_map/add | solution.py:198
  0.9 0.0 copy-start.3
  0.9 1.3 %copy-done.3 = bf16[256,2048]{1,0:T(8,128)(2,1)S(1)} copy-done((bf16[256,2048]{1,0:T(8,128)(2,1)S(1)}, bf16[256,2048]{1,0:T(8,128)(2,1)}, u32[]{:S(2)}) %copy-start.3) | copy-done | bytes 1048600
  2.2 1.1 %group_rows.1 = (bf16[256,256]{1,0:T(8,128)(2,1)S(1)}, bf16[64,2176]{1,0:T(8,128)(2,1)S(1)}, bf16[64,2176]{1,0:T(8,128)(2,1)S(1)}, bf16[64,2176]{1,0:T(8,128)(2,1)S(1)}, bf16[64,2176]{1,0:T(8,128)(2,1)S(1)}) custom-call(s32[1,256]{1,0:T(1,128)S(1)} %bitcast.4, bf16[256,2048]{1,0:T(8,128)(2,1)S(1)} %copy-done.3), custom_call_target="tpu_custom_call" | custom-call | tf_op jit(solution)/shard_map/group_rows/pallas_call | solution.py:190
  3.3 0.5 %collective-permute-start = (bf16[64,2176]{1,0:T(8,128)(2,1)S(1)}, bf16[64,2176]{1,0:T(8,128)(2,1)S(1)}, u32[]{:S(2)}, u32[]{:S(2)}) collective-permute-start(bf16[64,2176]{1,0:T(8,128)(2,1)S(1)} %get-tuple-element.32), channel_id=1, source_target_pairs={{0,4},{1,5},{2,6},{3,7},{4,0},{5,1},{6,2},{7,3},{8,12},{9,13},{10,... | collective-permute-start | bytes 835592 | tf_op jit(solution)/shard_map/ppermute | solution.py:188
  3.8 2.6 %collective-permute-start.7 = (bf16[64,2176]{1,0:T(8,128)(2,1)S(1)}, bf16[64,2176]{1,0:T(8,128)(2,1)S(1)}, u32[]{:S(2)}, u32[]{:S(2)}) collective-permute-start(bf16[64,2176]{1,0:T(8,128)(2,1)S(1)} %get-tuple-element.42), channel_id=1, source_target_pairs={{0,8},{1,9},{2,10},{3,11},{4,12},{5,13},{6,14},{7,15},{8,0},{9,1},... | collective-permute-start | bytes 835592 | tf_op jit(solution)/shard_map/ppermute | solution.py:188
  6.4 0.1 collective-permute-start.8
  6.4 0.0 collective-permute-done.refs_1_
  6.5 0.0 copy-start.2
  6.5 2.3 %low_products.2 = (f32[8,128]{1,0:T(8,128)S(1)}, f32[32,128]{1,0:T(8,128)S(1)}, f32[32,128]{1,0:T(8,128)S(1)}, f32[32,128]{1,0:T(8,128)S(1)}, f32[32,128]{1,0:T(8,128)S(1)}) custom-call(bf16[64,2176]{1,0:T(8,128)(2,1)S(1)} %get-tuple-element.31.refs_0_, bf16[64,2176]{1,0:T(8,128)(2,1)S(1)} %collective-permute-done.refs_1_, bf16[16,2048,128]{2,1,0:T(8,128)(2,1)} %refs_2_.7), custom_call_target="tpu_custom_call" | custom-call | flops 134217728 | bytes 2097152 | tf_op jit(solution)/shard_map/low_products/pallas_call | solution.py:218
  8.7 0.0 copy-start.1
  8.7 1.9 %collective-permute-start.1 = (f32[32,128]{1,0:T(8,128)S(1)}, f32[32,128]{1,0:T(8,128)S(1)}, u32[]{:S(2)}, u32[]{:S(2)}) collective-permute-start(f32[32,128]{1,0:T(8,128)S(1)} %get-tuple-element.35), channel_id=1, source_target_pairs={{0,1},{1,0},{2,3},{3,2},{4,5},{5,4},{6,7},{7,6},{8,9},{9,8},{10,11... | collective-permute-start | bytes 49160 | tf_op jit(solution)/shard_map/ppermute | solution.py:188
  10.6 2.6 %collective-permute-start.2 = (f32[32,128]{1,0:T(8,128)S(1)}, f32[32,128]{1,0:T(8,128)S(1)}, u32[]{:S(2)}, u32[]{:S(2)}) collective-permute-start(f32[32,128]{1,0:T(8,128)S(1)} %get-tuple-element.36), channel_id=1, source_target_pairs={{0,2},{1,3},{2,0},{3,1},{4,6},{5,7},{6,4},{7,5},{8,10},{9,11},{10,... | collective-permute-start | bytes 49160 | tf_op jit(solution)/shard_map/ppermute | solution.py:188
  13.2 0.0 collective-permute-start.3
  13.2 0.0 copy-done
  13.2 1.3 %base_products.2.base_ref = f32[128,2048]{1,0:T(8,128)S(1)} custom-call(bf16[64,2176]{1,0:T(8,128)(2,1)S(1)} %get-tuple-element.31.refs_0_, bf16[64,2176]{1,0:T(8,128)(2,1)S(1)} %collective-permute-done.refs_1_, bf16[2048,2048]{1,0:T(8,128)(2,1)S(1)} %copy-done), custom_call_target="tpu_custom_call" | custom-call | flops 1073741824 | bytes 8388608 | tf_op jit(solution)/shard_map/base_products/pallas_call | solution.py:244
  14.5 0.0 collective-permute-done.1.refs_1_
  14.5 0.7 %collective-permute-done.2.refs_2_ = f32[32,128]{1,0:T(8,128)S(1)} collective-permute-done((f32[32,128]{1,0:T(8,128)S(1)}, f32[32,128]{1,0:T(8,128)S(1)}, u32[]{:S(2)}, u32[]{:S(2)}) %collective-permute-start.2) | collective-permute-done | bytes 16416 | tf_op jit(solution)/shard_map/ppermute | solution.py:188
  15.3 3.5 %collective-permute-done.3.refs_3_ = f32[32,128]{1,0:T(8,128)S(1)} collective-permute-done((f32[32,128]{1,0:T(8,128)S(1)}, f32[32,128]{1,0:T(8,128)S(1)}, u32[]{:S(2)}, u32[]{:S(2)}) %collective-permute-start.3) | collective-permute-done | bytes 16416 | tf_op jit(solution)/shard_map/ppermute | solution.py:188
  18.7 0.0 copy-done.2
  18.8 0.4 up_products.2
  19.1 0.1 collective-permute-start.4
  19.2 0.7 %collective-permute-start.5 = (bf16[128,512]{1,0:T(8,128)(2,1)S(1)}, bf16[128,512]{1,0:T(8,128)(2,1)S(1)}, u32[]{:S(2)}, u32[]{:S(2)}) collective-permute-start(bf16[128,512]{1,0:T(8,128)(2,1)S(1)} %get-tuple-element.40), channel_id=1, source_target_pairs={{0,2},{1,3},{2,0},{3,1},{4,6},{5,7},{6,4},{7,5},{8,10},{9,11},{10,... | collective-permute-start | bytes 393224 | tf_op jit(solution)/shard_map/ppermute | solution.py:188
  19.9 0.0 collective-permute-done.7.refs_0_
  19.9 0.0 collective-permute-done.8.refs_1_
  19.9 0.0 copy-done.1
  20.0 0.8 %low_products.3 = (f32[8,128]{1,0:T(8,128)S(1)}, f32[32,128]{1,0:T(8,128)S(1)}, f32[32,128]{1,0:T(8,128)S(1)}, f32[32,128]{1,0:T(8,128)S(1)}, f32[32,128]{1,0:T(8,128)S(1)}) custom-call(bf16[64,2176]{1,0:T(8,128)(2,1)S(1)} %collective-permute-done.7.refs_0_, bf16[64,2176]{1,0:T(8,128)(2,1)S(1)} %collective-permute-done.8.refs_1_, ...), custom_call_target="tpu_custom_call" | custom-call | flops 134217728 | bytes 2097152 | tf_op jit(solution)/shard_map/low_products/pallas_call | solution.py:218
  20.7 1.4 %collective-permute-start.9 = (f32[32,128]{1,0:T(8,128)S(1)}, f32[32,128]{1,0:T(8,128)S(1)}, u32[]{:S(2)}, u32[]{:S(2)}) collective-permute-start(f32[32,128]{1,0:T(8,128)S(1)} %get-tuple-element.46), channel_id=1, source_target_pairs={{0,1},{1,0},{2,3},{3,2},{4,5},{5,4},{6,7},{7,6},{8,9},{9,8},{10,11... | collective-permute-start | bytes 49160 | tf_op jit(solution)/shard_map/ppermute | solution.py:188
  22.1 2.9 %collective-permute-start.10 = (f32[32,128]{1,0:T(8,128)S(1)}, f32[32,128]{1,0:T(8,128)S(1)}, u32[]{:S(2)}, u32[]{:S(2)}) collective-permute-start(f32[32,128]{1,0:T(8,128)S(1)} %get-tuple-element.47), channel_id=1, source_target_pairs={{0,2},{1,3},{2,0},{3,1},{4,6},{5,7},{6,4},{7,5},{8,10},{9,11},{10,... | collective-permute-start | bytes 49160 | tf_op jit(solution)/shard_map/ppermute | solution.py:188
  25.0 0.2 collective-permute-start.11
  25.2 1.3 %base_products.3.base_ref = f32[128,2048]{1,0:T(8,128)S(1)} custom-call(bf16[64,2176]{1,0:T(8,128)(2,1)S(1)} %collective-permute-done.7.refs_0_, bf16[64,2176]{1,0:T(8,128)(2,1)S(1)} %collective-permute-done.8.refs_1_, bf16[2048,2048]{1,0:T(8,128)(2,1)S(1)} %copy-done), custom_call_target="tpu_custom_call" | custom-call | flops 1073741824 | bytes 8388608 | tf_op jit(solution)/shard_map/base_products/pallas_call | solution.py:244
  26.5 0.0 collective-permute-done.9.refs_1_
  26.5 3.7 %collective-permute-start.6 = (bf16[128,512]{1,0:T(8,128)(2,1)S(1)}, bf16[128,512]{1,0:T(8,128)(2,1)S(1)}, u32[]{:S(2)}, u32[]{:S(2)}) collective-permute-start(bf16[128,512]{1,0:T(8,128)(2,1)S(1)} %get-tuple-element.41.refs_3_), channel_id=1, source_target_pairs={{0,3},{1,2},{2,1},{3,0},{4,7},{5,6},{6,5},{7,4},{8,11},{9,10},{10,... | collective-permute-start | bytes 393224 | tf_op jit(solution)/shard_map/ppermute | solution.py:188
  30.2 0.0 collective-permute-done.10.refs_2_
  30.2 0.6 %collective-permute-done.11.refs_3_ = f32[32,128]{1,0:T(8,128)S(1)} collective-permute-done((f32[32,128]{1,0:T(8,128)S(1)}, f32[32,128]{1,0:T(8,128)S(1)}, u32[]{:S(2)}, u32[]{:S(2)}) %collective-permute-start.11) | collective-permute-done | bytes 16416 | tf_op jit(solution)/shard_map/ppermute | solution.py:188
  30.8 0.4 up_products.3
  31.2 1.5 %collective-permute-start.12 = (bf16[128,512]{1,0:T(8,128)(2,1)S(1)}, bf16[128,512]{1,0:T(8,128)(2,1)S(1)}, u32[]{:S(2)}, u32[]{:S(2)}) collective-permute-start(bf16[128,512]{1,0:T(8,128)(2,1)S(1)} %get-tuple-element.49), channel_id=1, source_target_pairs={{0,8},{1,9},{2,10},{3,11},{4,12},{5,13},{6,14},{7,15},{8,0},{9,1},... | collective-permute-start | bytes 393224 | tf_op jit(solution)/shard_map/ppermute | solution.py:188
  32.7 0.0 collective-permute-start.13
  32.8 0.0 collective-permute-done.4.refs_1_
  32.8 1.4 %collective-permute-start.14 = (bf16[128,512]{1,0:T(8,128)(2,1)S(1)}, bf16[128,512]{1,0:T(8,128)(2,1)S(1)}, u32[]{:S(2)}, u32[]{:S(2)}) collective-permute-start(bf16[128,512]{1,0:T(8,128)(2,1)S(1)} %get-tuple-element.51), channel_id=1, source_target_pairs={{0,10},{1,11},{2,8},{3,9},{4,14},{5,15},{6,12},{7,13},{8,2},{9,3},... | collective-permute-start | bytes 393224 | tf_op jit(solution)/shard_map/ppermute | solution.py:188
  34.2 0.0 collective-permute-done.5.refs_2_
  34.2 3.9 %collective-permute-start.15 = (bf16[128,512]{1,0:T(8,128)(2,1)S(1)}, bf16[128,512]{1,0:T(8,128)(2,1)S(1)}, u32[]{:S(2)}, u32[]{:S(2)}) collective-permute-start(bf16[128,512]{1,0:T(8,128)(2,1)S(1)} %get-tuple-element.52), channel_id=1, source_target_pairs={{0,11},{1,10},{2,9},{3,8},{4,15},{5,14},{6,13},{7,12},{8,3},{9,2},... | collective-permute-start | bytes 393224 | tf_op jit(solution)/shard_map/ppermute | solution.py:188
  38.0 0.0 collective-permute-done.6.refs_3_
  38.0 3.5 %collective-permute-done.12.refs_4_ = bf16[128,512]{1,0:T(8,128)(2,1)S(1)} collective-permute-done((bf16[128,512]{1,0:T(8,128)(2,1)S(1)}, bf16[128,512]{1,0:T(8,128)(2,1)S(1)}, u32[]{:S(2)}, u32[]{:S(2)}) %collective-permute-start.12) | collective-permute-done | bytes 131104 | tf_op jit(solution)/shard_map/ppermute | solution.py:188
  41.6 0.0 collective-permute-done.13.refs_5_
  41.6 3.8 %collective-permute-done.14.refs_6_ = bf16[128,512]{1,0:T(8,128)(2,1)S(1)} collective-permute-done((bf16[128,512]{1,0:T(8,128)(2,1)S(1)}, bf16[128,512]{1,0:T(8,128)(2,1)S(1)}, u32[]{:S(2)}, u32[]{:S(2)}) %collective-permute-start.14) | collective-permute-done | bytes 131104 | tf_op jit(solution)/shard_map/ppermute | solution.py:188
  45.3 0.0 collective-permute-done.15.refs_7_
  45.3 0.1 sums.1
  45.5 0.1 collective-permute-start.16
  45.6 1.3 %collective-permute-done.16.refs_1_ = bf16[128,512]{1,0:T(8,128)(2,1)S(1)} collective-permute-done((bf16[128,512]{1,0:T(8,128)(2,1)S(1)}, bf16[128,512]{1,0:T(8,128)(2,1)S(1)}, u32[]{:S(2)}, u32[]{:S(2)}) %collective-permute-start.16) | collective-permute-done | bytes 131104 | tf_op jit(solution)/shard_map/ppermute | solution.py:188
  46.9 1.0 %finish.1 = bf16[256,512]{1,0:T(8,128)(2,1)} custom-call(bf16[256,256]{1,0:T(8,128)(2,1)S(1)} %get-tuple-element.30.place_ref, bf16[128,512]{1,0:T(8,128)(2,1)S(1)} %get-tuple-element.53.refs_0_, bf16[128,512]{1,0:T(8,128)(2,1)S(1)} %collective-permute-done.16.refs_1_), custom_call_target="tpu_custom_call" | custom-call | tf_op jit(solution)/shard_map/finish/pallas_call | solution.py:304
Async XLA Ops:
  0.0 13.2 %copy-start = (bf16[2048,2048]{1,0:T(8,128)(2,1)S(1)}, bf16[2048,2048]{1,0:T(8,128)(2,1)}, u32[]{:S(2)}) copy-start(bf16[2048,2048]{1,0:T(8,128)(2,1)} %refs_2_.6) | copy-start | bytes 25165828
  0.9 1.3 %copy-start.3 = (bf16[256,2048]{1,0:T(8,128)(2,1)S(1)}, bf16[256,2048]{1,0:T(8,128)(2,1)}, u32[]{:S(2)}) copy-start(bf16[256,2048]{1,0:T(8,128)(2,1)} %tokens_ref.1) | copy-start | bytes 3145732
  3.3 3.1 %collective-permute-start = (bf16[64,2176]{1,0:T(8,128)(2,1)S(1)}, bf16[64,2176]{1,0:T(8,128)(2,1)S(1)}, u32[]{:S(2)}, u32[]{:S(2)}) collective-permute-start(bf16[64,2176]{1,0:T(8,128)(2,1)S(1)} %get-tuple-element.32), channel_id=1, source_target_pairs={{0,4},{1,5},{2,6},{3,7},{4,0},{5,1},{6,2},{7,3},{8,12},{9,13},{10,... | collective-permute-start | bytes 835592 | tf_op jit(solution)/shard_map/ppermute | solution.py:188
  3.8 16.1 %collective-permute-start.7 = (bf16[64,2176]{1,0:T(8,128)(2,1)S(1)}, bf16[64,2176]{1,0:T(8,128)(2,1)S(1)}, u32[]{:S(2)}, u32[]{:S(2)}) collective-permute-start(bf16[64,2176]{1,0:T(8,128)(2,1)S(1)} %get-tuple-element.42), channel_id=1, source_target_pairs={{0,8},{1,9},{2,10},{3,11},{4,12},{5,13},{6,14},{7,15},{8,0},{9,1},... | collective-permute-start | bytes 835592 | tf_op jit(solution)/shard_map/ppermute | solution.py:188
  6.4 13.6 %collective-permute-start.8 = (bf16[64,2176]{1,0:T(8,128)(2,1)S(1)}, bf16[64,2176]{1,0:T(8,128)(2,1)S(1)}, u32[]{:S(2)}, u32[]{:S(2)}) collective-permute-start(bf16[64,2176]{1,0:T(8,128)(2,1)S(1)} %get-tuple-element.43), channel_id=1, source_target_pairs={{0,12},{1,13},{2,14},{3,15},{4,8},{5,9},{6,10},{7,11},{8,4},{9,5},... | collective-permute-start | bytes 835592 | tf_op jit(solution)/shard_map/ppermute | solution.py:188
  6.5 12.3 %copy-start.2 = (bf16[16,16,2048]{2,1,0:T(8,128)(2,1)S(1)}, bf16[16,16,2048]{2,1,0:T(8,128)(2,1)}, u32[]{:S(2)}) copy-start(bf16[16,16,2048]{2,1,0:T(8,128)(2,1)} %param.9) | copy-start | bytes 3145732
  8.7 11.2 %copy-start.1 = (bf16[16,2048,128]{2,1,0:T(8,128)(2,1)S(1)}, bf16[16,2048,128]{2,1,0:T(8,128)(2,1)}, u32[]{:S(2)}) copy-start(bf16[16,2048,128]{2,1,0:T(8,128)(2,1)} %refs_2_.7) | copy-start | bytes 25165828
  8.7 5.8 %collective-permute-start.1 = (f32[32,128]{1,0:T(8,128)S(1)}, f32[32,128]{1,0:T(8,128)S(1)}, u32[]{:S(2)}, u32[]{:S(2)}) collective-permute-start(f32[32,128]{1,0:T(8,128)S(1)} %get-tuple-element.35), channel_id=1, source_target_pairs={{0,1},{1,0},{2,3},{3,2},{4,5},{5,4},{6,7},{7,6},{8,9},{9,8},{10,11... | collective-permute-start | bytes 49160 | tf_op jit(solution)/shard_map/ppermute | solution.py:188
  10.6 4.6 %collective-permute-start.2 = (f32[32,128]{1,0:T(8,128)S(1)}, f32[32,128]{1,0:T(8,128)S(1)}, u32[]{:S(2)}, u32[]{:S(2)}) collective-permute-start(f32[32,128]{1,0:T(8,128)S(1)} %get-tuple-element.36), channel_id=1, source_target_pairs={{0,2},{1,3},{2,0},{3,1},{4,6},{5,7},{6,4},{7,5},{8,10},{9,11},{10,... | collective-permute-start | bytes 49160 | tf_op jit(solution)/shard_map/ppermute | solution.py:188
  13.2 5.5 %collective-permute-start.3 = (f32[32,128]{1,0:T(8,128)S(1)}, f32[32,128]{1,0:T(8,128)S(1)}, u32[]{:S(2)}, u32[]{:S(2)}) collective-permute-start(f32[32,128]{1,0:T(8,128)S(1)} %get-tuple-element.37), channel_id=1, source_target_pairs={{0,3},{1,2},{2,1},{3,0},{4,7},{5,6},{6,5},{7,4},{8,11},{9,10},{10,... | collective-permute-start | bytes 49160 | tf_op jit(solution)/shard_map/ppermute | solution.py:188
  19.1 13.6 %collective-permute-start.4 = (bf16[128,512]{1,0:T(8,128)(2,1)S(1)}, bf16[128,512]{1,0:T(8,128)(2,1)S(1)}, u32[]{:S(2)}, u32[]{:S(2)}) collective-permute-start(bf16[128,512]{1,0:T(8,128)(2,1)S(1)} %get-tuple-element.39), channel_id=1, source_target_pairs={{0,1},{1,0},{2,3},{3,2},{4,5},{5,4},{6,7},{7,6},{8,9},{9,8},{10,11... | collective-permute-start | bytes 393224 | tf_op jit(solution)/shard_map/ppermute | solution.py:188
  19.2 15.0 %collective-permute-start.5 = (bf16[128,512]{1,0:T(8,128)(2,1)S(1)}, bf16[128,512]{1,0:T(8,128)(2,1)S(1)}, u32[]{:S(2)}, u32[]{:S(2)}) collective-permute-start(bf16[128,512]{1,0:T(8,128)(2,1)S(1)} %get-tuple-element.40), channel_id=1, source_target_pairs={{0,2},{1,3},{2,0},{3,1},{4,6},{5,7},{6,4},{7,5},{8,10},{9,11},{10,... | collective-permute-start | bytes 393224 | tf_op jit(solution)/shard_map/ppermute | solution.py:188
  20.7 5.7 %collective-permute-start.9 = (f32[32,128]{1,0:T(8,128)S(1)}, f32[32,128]{1,0:T(8,128)S(1)}, u32[]{:S(2)}, u32[]{:S(2)}) collective-permute-start(f32[32,128]{1,0:T(8,128)S(1)} %get-tuple-element.46), channel_id=1, source_target_pairs={{0,1},{1,0},{2,3},{3,2},{4,5},{5,4},{6,7},{7,6},{8,9},{9,8},{10,11... | collective-permute-start | bytes 49160 | tf_op jit(solution)/shard_map/ppermute | solution.py:188
  22.1 8.1 %collective-permute-start.10 = (f32[32,128]{1,0:T(8,128)S(1)}, f32[32,128]{1,0:T(8,128)S(1)}, u32[]{:S(2)}, u32[]{:S(2)}) collective-permute-start(f32[32,128]{1,0:T(8,128)S(1)} %get-tuple-element.47), channel_id=1, source_target_pairs={{0,2},{1,3},{2,0},{3,1},{4,6},{5,7},{6,4},{7,5},{8,10},{9,11},{10,... | collective-permute-start | bytes 49160 | tf_op jit(solution)/shard_map/ppermute | solution.py:188
  25.0 5.8 %collective-permute-start.11 = (f32[32,128]{1,0:T(8,128)S(1)}, f32[32,128]{1,0:T(8,128)S(1)}, u32[]{:S(2)}, u32[]{:S(2)}) collective-permute-start(f32[32,128]{1,0:T(8,128)S(1)} %get-tuple-element.48), channel_id=1, source_target_pairs={{0,3},{1,2},{2,1},{3,0},{4,7},{5,6},{6,5},{7,4},{8,11},{9,10},{10,... | collective-permute-start | bytes 49160 | tf_op jit(solution)/shard_map/ppermute | solution.py:188
  26.5 11.6 %collective-permute-start.6 = (bf16[128,512]{1,0:T(8,128)(2,1)S(1)}, bf16[128,512]{1,0:T(8,128)(2,1)S(1)}, u32[]{:S(2)}, u32[]{:S(2)}) collective-permute-start(bf16[128,512]{1,0:T(8,128)(2,1)S(1)} %get-tuple-element.41.refs_3_), channel_id=1, source_target_pairs={{0,3},{1,2},{2,1},{3,0},{4,7},{5,6},{6,5},{7,4},{8,11},{9,10},{10,... | collective-permute-start | bytes 393224 | tf_op jit(solution)/shard_map/ppermute | solution.py:188
  31.2 10.3 %collective-permute-start.12 = (bf16[128,512]{1,0:T(8,128)(2,1)S(1)}, bf16[128,512]{1,0:T(8,128)(2,1)S(1)}, u32[]{:S(2)}, u32[]{:S(2)}) collective-permute-start(bf16[128,512]{1,0:T(8,128)(2,1)S(1)} %get-tuple-element.49), channel_id=1, source_target_pairs={{0,8},{1,9},{2,10},{3,11},{4,12},{5,13},{6,14},{7,15},{8,0},{9,1},... | collective-permute-start | bytes 393224 | tf_op jit(solution)/shard_map/ppermute | solution.py:188
  32.7 8.8 %collective-permute-start.13 = (bf16[128,512]{1,0:T(8,128)(2,1)S(1)}, bf16[128,512]{1,0:T(8,128)(2,1)S(1)}, u32[]{:S(2)}, u32[]{:S(2)}) collective-permute-start(bf16[128,512]{1,0:T(8,128)(2,1)S(1)} %get-tuple-element.50), channel_id=1, source_target_pairs={{0,9},{1,8},{2,11},{3,10},{4,13},{5,12},{6,15},{7,14},{8,1},{9,0},... | collective-permute-start | bytes 393224 | tf_op jit(solution)/shard_map/ppermute | solution.py:188
  32.8 12.6 %collective-permute-start.14 = (bf16[128,512]{1,0:T(8,128)(2,1)S(1)}, bf16[128,512]{1,0:T(8,128)(2,1)S(1)}, u32[]{:S(2)}, u32[]{:S(2)}) collective-permute-start(bf16[128,512]{1,0:T(8,128)(2,1)S(1)} %get-tuple-element.51), channel_id=1, source_target_pairs={{0,10},{1,11},{2,8},{3,9},{4,14},{5,15},{6,12},{7,13},{8,2},{9,3},... | collective-permute-start | bytes 393224 | tf_op jit(solution)/shard_map/ppermute | solution.py:188
  34.2 11.2 %collective-permute-start.15 = (bf16[128,512]{1,0:T(8,128)(2,1)S(1)}, bf16[128,512]{1,0:T(8,128)(2,1)S(1)}, u32[]{:S(2)}, u32[]{:S(2)}) collective-permute-start(bf16[128,512]{1,0:T(8,128)(2,1)S(1)} %get-tuple-element.52), channel_id=1, source_target_pairs={{0,11},{1,10},{2,9},{3,8},{4,15},{5,14},{6,13},{7,12},{8,3},{9,2},... | collective-permute-start | bytes 393224 | tf_op jit(solution)/shard_map/ppermute | solution.py:188
  45.5 1.4 %collective-permute-start.16 = (bf16[128,512]{1,0:T(8,128)(2,1)S(1)}, bf16[128,512]{1,0:T(8,128)(2,1)S(1)}, u32[]{:S(2)}, u32[]{:S(2)}) collective-permute-start(bf16[128,512]{1,0:T(8,128)(2,1)S(1)} %get-tuple-element.54), channel_id=1, source_target_pairs={{0,4},{1,5},{2,6},{3,7},{4,0},{5,1},{6,2},{7,3},{8,12},{9,13},{10,... | collective-permute-start | bytes 393224 | tf_op jit(solution)/shard_map/ppermute | solution.py:188

commit v4 on v3

--- a/solution.py
+++ b/solution.py
@@ -16,6 +16,8 @@
 ANY = pl.BlockSpec(memory_space=pl.ANY)
 PARAMS = pltpu.CompilerParams(vmem_limit_bytes=16 * 1024 * 1024)
 WIDE = pltpu.CompilerParams(vmem_limit_bytes=48 * 1024 * 1024)
+ORDER = ((3, 2, 1, 0), (0, 2, 3, 1))
+LOW_ORDER = ((0, 2, 3, 1), (0, 1, 2, 3))
 TWO_STEP_LOW = (False, False)
 TWO_STEP_SHARES = (False, False)
 
@@ -240,7 +242,8 @@
                 got = swap(send, 0, distance)
             pieces = [keep, got]
         else:
-            pieces = [swap(value, 0, j) if j else value for j, value in enumerate(pieces)]
+            order = LOW_ORDER[bool(after)] if tensor_count == 4 else range(tensor_count)
+            pieces = [swap(pieces[j], 0, j) if j else pieces[j] for j in order]
         base = pl.pallas_call(
             functools.partial(base_kernel, count),
             out_shape=shape((part_rows, columns), F32),
@@ -281,8 +284,8 @@
                     got = swap(send, k if last else 0, distance)
                 received.append([swap(keep, k, 0) if k else keep, got])
             elif store_count * tensor_count <= 16:
-                blocks = [swap(mine[j], k, j) if k or j else mine[j] for j in reversed(range(tensor_count))]
-                received.append(blocks[::-1])
+                blocks = [swap(mine[j], k, j) if k or j else mine[j] for j in (ORDER[bool(k)] if tensor_count == 4 else range(tensor_count))]
+                received.append(blocks)
             else:
                 order = jnp.arange(tensor_count, dtype=jnp.int32) ^ lax.axis_index("tensor")
                 stacked = jnp.take(jnp.stack(mine), order, axis=0)

time: 48 us -> 46.8 us (0.975)
  waiting for transfers between devices: 13.5 us -> 12.2 us
    ppermute x17, waiting for transfers between devices: 13.5 us -> 12.2 us  [swap(): return lax.ppermute(value, ('store', 'tensor'), pairs)]
  transfers between devices with their start and end apart: 17 -> 17, of which waited for: 6 -> 6; matrix products, arithmetic and copies ran while one was open for 0% -> 0% of each run, Pallas kernels for 13% -> 14%
where the time goes in v4:
time: 46.8 us; the launch traced here: 46.6 us
  starting transfers between devices  23.6 us (50%)
  waiting for transfers between devices  12.2 us (26%)
  Pallas kernels  8.53 us (18%)
  local copies, waits for them, and re-layouts  1.36 us (3%)
  other arithmetic  0.85 us (2%)
    ppermute x17, starting transfers between devices, swap(): return lax.ppermute(value, ('store', 'tensor'), pairs)  23.6 us
    ppermute x17, waiting for transfers between devices, swap(): return lax.ppermute(value, ('store', 'tensor'), pairs)  12.2 us
    pallas_call x2, Pallas kernels, shards(): pl.pallas_call(functools.partial(down_kernel, count, tensor_count, len(af...  3.04 us
    pallas_call x2, Pallas kernels, shards(): pl.pallas_call(functools.partial(base_kernel, count), out_shape=shape((pa...  2.54 us
    unnamed x8, local copies, waits for them, and re-layouts  1.36 us
    pallas_call x1, Pallas kernels, shards(): pl.pallas_call(functools.partial(group_kernel, store_count, adapters), ou...  1.12 us
    pallas_call x1, Pallas kernels, shards(): pl.pallas_call(functools.partial(finish_kernel, both), out_shape=shape((r...  0.95 us
  transfers between devices with their start and end apart: 17, of which 6 were waited for; matrix products, arithmetic and copies ran while one was open for 0% of the time, Pallas kernels for 14%

profile of v4, /device:TPU:0, one launch (start us, length us, event | category | flops | bytes accessed | tf_op | source)
XLA Modules:
  0.0 46.6 jit_solution(7047398562929989105)
XLA Ops:
  0.0 0.0 copy-start
  0.0 0.8 %multiply_add_fusion = s32[256]{0:T(256)S(1)} fusion(s32[256]{0:T(256)} %param.10, s32[256]{0:T(256)} %param.11), kind=kLoop, calls=%fused_computation | loop fusion | flops 512 | bytes 3072 | tf_op jit(solution)/shard_map/add | solution.py:200
  0.9 0.0 copy-start.3
  0.9 1.3 %copy-done.3 = bf16[256,2048]{1,0:T(8,128)(2,1)S(1)} copy-done((bf16[256,2048]{1,0:T(8,128)(2,1)S(1)}, bf16[256,2048]{1,0:T(8,128)(2,1)}, u32[]{:S(2)}) %copy-start.3) | copy-done | bytes 1048600
  2.2 1.1 %group_rows.1 = (bf16[256,256]{1,0:T(8,128)(2,1)S(1)}, bf16[64,2176]{1,0:T(8,128)(2,1)S(1)}, bf16[64,2176]{1,0:T(8,128)(2,1)S(1)}, bf16[64,2176]{1,0:T(8,128)(2,1)S(1)}, bf16[64,2176]{1,0:T(8,128)(2,1)S(1)}) custom-call(s32[1,256]{1,0:T(1,128)S(1)} %bitcast.4, bf16[256,2048]{1,0:T(8,128)(2,1)S(1)} %copy-done.3), custom_call_target="tpu_custom_call" | custom-call | tf_op jit(solution)/shard_map/group_rows/pallas_call | solution.py:192
  3.3 0.5 %collective-permute-start = (bf16[64,2176]{1,0:T(8,128)(2,1)S(1)}, bf16[64,2176]{1,0:T(8,128)(2,1)S(1)}, u32[]{:S(2)}, u32[]{:S(2)}) collective-permute-start(bf16[64,2176]{1,0:T(8,128)(2,1)S(1)} %get-tuple-element.32), channel_id=1, source_target_pairs={{0,4},{1,5},{2,6},{3,7},{4,0},{5,1},{6,2},{7,3},{8,12},{9,13},{10,... | collective-permute-start | bytes 835592 | tf_op jit(solution)/shard_map/ppermute | solution.py:190
  3.8 2.6 %collective-permute-start.7 = (bf16[64,2176]{1,0:T(8,128)(2,1)S(1)}, bf16[64,2176]{1,0:T(8,128)(2,1)S(1)}, u32[]{:S(2)}, u32[]{:S(2)}) collective-permute-start(bf16[64,2176]{1,0:T(8,128)(2,1)S(1)} %get-tuple-element.42), channel_id=1, source_target_pairs={{0,8},{1,9},{2,10},{3,11},{4,12},{5,13},{6,14},{7,15},{8,0},{9,1},... | collective-permute-start | bytes 835592 | tf_op jit(solution)/shard_map/ppermute | solution.py:190
  6.4 0.1 collective-permute-start.8
  6.4 0.0 collective-permute-done.refs_1_
  6.5 0.0 copy-start.2
  6.5 2.3 %low_products.2 = (f32[8,128]{1,0:T(8,128)S(1)}, f32[32,128]{1,0:T(8,128)S(1)}, f32[32,128]{1,0:T(8,128)S(1)}, f32[32,128]{1,0:T(8,128)S(1)}, f32[32,128]{1,0:T(8,128)S(1)}) custom-call(bf16[64,2176]{1,0:T(8,128)(2,1)S(1)} %get-tuple-element.31.refs_0_, bf16[64,2176]{1,0:T(8,128)(2,1)S(1)} %collective-permute-done.refs_1_, bf16[16,2048,128]{2,1,0:T(8,128)(2,1)} %refs_2_.7), custom_call_target="tpu_custom_call" | custom-call | flops 134217728 | bytes 2097152 | tf_op jit(solution)/shard_map/low_products/pallas_call | solution.py:220
  8.7 0.0 copy-start.1
  8.7 2.9 %collective-permute-start.1 = (f32[32,128]{1,0:T(8,128)S(1)}, f32[32,128]{1,0:T(8,128)S(1)}, u32[]{:S(2)}, u32[]{:S(2)}) collective-permute-start(f32[32,128]{1,0:T(8,128)S(1)} %get-tuple-element.35), channel_id=1, source_target_pairs={{0,2},{1,3},{2,0},{3,1},{4,6},{5,7},{6,4},{7,5},{8,10},{9,11},{10,... | collective-permute-start | bytes 49160 | tf_op jit(solution)/shard_map/ppermute | solution.py:190
  11.6 1.4 %collective-permute-start.2 = (f32[32,128]{1,0:T(8,128)S(1)}, f32[32,128]{1,0:T(8,128)S(1)}, u32[]{:S(2)}, u32[]{:S(2)}) collective-permute-start(f32[32,128]{1,0:T(8,128)S(1)} %get-tuple-element.36), channel_id=1, source_target_pairs={{0,3},{1,2},{2,1},{3,0},{4,7},{5,6},{6,5},{7,4},{8,11},{9,10},{10,... | collective-permute-start | bytes 49160 | tf_op jit(solution)/shard_map/ppermute | solution.py:190
  13.0 0.2 collective-permute-start.3
  13.2 0.0 copy-done
  13.2 1.3 %base_products.2.base_ref = f32[128,2048]{1,0:T(8,128)S(1)} custom-call(bf16[64,2176]{1,0:T(8,128)(2,1)S(1)} %get-tuple-element.31.refs_0_, bf16[64,2176]{1,0:T(8,128)(2,1)S(1)} %collective-permute-done.refs_1_, bf16[2048,2048]{1,0:T(8,128)(2,1)S(1)} %copy-done), custom_call_target="tpu_custom_call" | custom-call | flops 1073741824 | bytes 8388608 | tf_op jit(solution)/shard_map/base_products/pallas_call | solution.py:247
  14.5 0.0 collective-permute-done.1.refs_1_
  14.5 2.7 %collective-permute-done.2.refs_2_ = f32[32,128]{1,0:T(8,128)S(1)} collective-permute-done((f32[32,128]{1,0:T(8,128)S(1)}, f32[32,128]{1,0:T(8,128)S(1)}, u32[]{:S(2)}, u32[]{:S(2)}) %collective-permute-start.2) | collective-permute-done | bytes 16416 | tf_op jit(solution)/shard_map/ppermute | solution.py:190
  17.2 0.0 collective-permute-done.3.refs_3_
  17.2 0.0 copy-done.2
  17.2 0.4 up_products.2
  17.5 1.3 %collective-permute-start.5 = (bf16[128,512]{1,0:T(8,128)(2,1)S(1)}, bf16[128,512]{1,0:T(8,128)(2,1)S(1)}, u32[]{:S(2)}, u32[]{:S(2)}) collective-permute-start(bf16[128,512]{1,0:T(8,128)(2,1)S(1)} %get-tuple-element.39), channel_id=1, source_target_pairs={{0,2},{1,3},{2,0},{3,1},{4,6},{5,7},{6,4},{7,5},{8,10},{9,11},{10,... | collective-permute-start | bytes 393224 | tf_op jit(solution)/shard_map/ppermute | solution.py:190
  18.9 1.3 %collective-permute-start.6 = (bf16[128,512]{1,0:T(8,128)(2,1)S(1)}, bf16[128,512]{1,0:T(8,128)(2,1)S(1)}, u32[]{:S(2)}, u32[]{:S(2)}) collective-permute-start(bf16[128,512]{1,0:T(8,128)(2,1)S(1)} %get-tuple-element.40), channel_id=1, source_target_pairs={{0,1},{1,0},{2,3},{3,2},{4,5},{5,4},{6,7},{7,6},{8,9},{9,8},{10,11... | collective-permute-start | bytes 393224 | tf_op jit(solution)/shard_map/ppermute | solution.py:190
  20.2 0.0 collective-permute-done.7.refs_0_
  20.2 0.0 collective-permute-done.8.refs_1_
  20.2 0.0 copy-done.1
  20.2 0.8 %low_products.3 = (f32[8,128]{1,0:T(8,128)S(1)}, f32[32,128]{1,0:T(8,128)S(1)}, f32[32,128]{1,0:T(8,128)S(1)}, f32[32,128]{1,0:T(8,128)S(1)}, f32[32,128]{1,0:T(8,128)S(1)}) custom-call(bf16[64,2176]{1,0:T(8,128)(2,1)S(1)} %collective-permute-done.7.refs_0_, bf16[64,2176]{1,0:T(8,128)(2,1)S(1)} %collective-permute-done.8.refs_1_, ...), custom_call_target="tpu_custom_call" | custom-call | flops 134217728 | bytes 2097152 | tf_op jit(solution)/shard_map/low_products/pallas_call | solution.py:220
  21.0 0.8 %collective-permute-start.9 = (f32[32,128]{1,0:T(8,128)S(1)}, f32[32,128]{1,0:T(8,128)S(1)}, u32[]{:S(2)}, u32[]{:S(2)}) collective-permute-start(f32[32,128]{1,0:T(8,128)S(1)} %get-tuple-element.46), channel_id=1, source_target_pairs={{0,1},{1,0},{2,3},{3,2},{4,5},{5,4},{6,7},{7,6},{8,9},{9,8},{10,11... | collective-permute-start | bytes 49160 | tf_op jit(solution)/shard_map/ppermute | solution.py:190
  21.8 2.6 %collective-permute-start.10 = (f32[32,128]{1,0:T(8,128)S(1)}, f32[32,128]{1,0:T(8,128)S(1)}, u32[]{:S(2)}, u32[]{:S(2)}) collective-permute-start(f32[32,128]{1,0:T(8,128)S(1)} %get-tuple-element.47), channel_id=1, source_target_pairs={{0,2},{1,3},{2,0},{3,1},{4,6},{5,7},{6,4},{7,5},{8,10},{9,11},{10,... | collective-permute-start | bytes 49160 | tf_op jit(solution)/shard_map/ppermute | solution.py:190
  24.4 1.0 %collective-permute-start.11 = (f32[32,128]{1,0:T(8,128)S(1)}, f32[32,128]{1,0:T(8,128)S(1)}, u32[]{:S(2)}, u32[]{:S(2)}) collective-permute-start(f32[32,128]{1,0:T(8,128)S(1)} %get-tuple-element.48), channel_id=1, source_target_pairs={{0,3},{1,2},{2,1},{3,0},{4,7},{5,6},{6,5},{7,4},{8,11},{9,10},{10,... | collective-permute-start | bytes 49160 | tf_op jit(solution)/shard_map/ppermute | solution.py:190
  25.4 1.3 %base_products.3.base_ref = f32[128,2048]{1,0:T(8,128)S(1)} custom-call(bf16[64,2176]{1,0:T(8,128)(2,1)S(1)} %collective-permute-done.7.refs_0_, bf16[64,2176]{1,0:T(8,128)(2,1)S(1)} %collective-permute-done.8.refs_1_, bf16[2048,2048]{1,0:T(8,128)(2,1)S(1)} %copy-done), custom_call_target="tpu_custom_call" | custom-call | flops 1073741824 | bytes 8388608 | tf_op jit(solution)/shard_map/base_products/pallas_call | solution.py:247
  26.7 0.0 collective-permute-done.9.refs_1_
  26.7 2.9 %collective-permute-start.4 = (bf16[128,512]{1,0:T(8,128)(2,1)S(1)}, bf16[128,512]{1,0:T(8,128)(2,1)S(1)}, u32[]{:S(2)}, u32[]{:S(2)}) collective-permute-start(bf16[128,512]{1,0:T(8,128)(2,1)S(1)} %get-tuple-element.38.refs_3_), channel_id=1, source_target_pairs={{0,3},{1,2},{2,1},{3,0},{4,7},{5,6},{6,5},{7,4},{8,11},{9,10},{10,... | collective-permute-start | bytes 393224 | tf_op jit(solution)/shard_map/ppermute | solution.py:190
  29.6 0.0 collective-permute-done.10.refs_2_
  29.6 0.6 %collective-permute-done.11.refs_3_ = f32[32,128]{1,0:T(8,128)S(1)} collective-permute-done((f32[32,128]{1,0:T(8,128)S(1)}, f32[32,128]{1,0:T(8,128)S(1)}, u32[]{:S(2)}, u32[]{:S(2)}) %collective-permute-start.11) | collective-permute-done | bytes 16416 | tf_op jit(solution)/shard_map/ppermute | solution.py:190
  30.1 0.4 up_products.3
  30.5 1.6 %collective-permute-start.12 = (bf16[128,512]{1,0:T(8,128)(2,1)S(1)}, bf16[128,512]{1,0:T(8,128)(2,1)S(1)}, u32[]{:S(2)}, u32[]{:S(2)}) collective-permute-start(bf16[128,512]{1,0:T(8,128)(2,1)S(1)} %get-tuple-element.49), channel_id=1, source_target_pairs={{0,8},{1,9},{2,10},{3,11},{4,12},{5,13},{6,14},{7,15},{8,0},{9,1},... | collective-permute-start | bytes 393224 | tf_op jit(solution)/shard_map/ppermute | solution.py:190
  32.1 0.0 collective-permute-start.13
  32.1 0.0 collective-permute-done.5.refs_1_
  32.1 1.7 %collective-permute-start.14 = (bf16[128,512]{1,0:T(8,128)(2,1)S(1)}, bf16[128,512]{1,0:T(8,128)(2,1)S(1)}, u32[]{:S(2)}, u32[]{:S(2)}) collective-permute-start(bf16[128,512]{1,0:T(8,128)(2,1)S(1)} %get-tuple-element.51), channel_id=1, source_target_pairs={{0,11},{1,10},{2,9},{3,8},{4,15},{5,14},{6,13},{7,12},{8,3},{9,2},... | collective-permute-start | bytes 393224 | tf_op jit(solution)/shard_map/ppermute | solution.py:190
  33.8 0.0 collective-permute-done.6.refs_2_
  33.8 2.6 %collective-permute-start.15 = (bf16[128,512]{1,0:T(8,128)(2,1)S(1)}, bf16[128,512]{1,0:T(8,128)(2,1)S(1)}, u32[]{:S(2)}, u32[]{:S(2)}) collective-permute-start(bf16[128,512]{1,0:T(8,128)(2,1)S(1)} %get-tuple-element.52), channel_id=1, source_target_pairs={{0,9},{1,8},{2,11},{3,10},{4,13},{5,12},{6,15},{7,14},{8,1},{9,0},... | collective-permute-start | bytes 393224 | tf_op jit(solution)/shard_map/ppermute | solution.py:190
  36.5 0.0 collective-permute-done.4.refs_0_
  36.5 6.6 %collective-permute-done.12.refs_4_ = bf16[128,512]{1,0:T(8,128)(2,1)S(1)} collective-permute-done((bf16[128,512]{1,0:T(8,128)(2,1)S(1)}, bf16[128,512]{1,0:T(8,128)(2,1)S(1)}, u32[]{:S(2)}, u32[]{:S(2)}) %collective-permute-start.12) | collective-permute-done | bytes 131104 | tf_op jit(solution)/shard_map/ppermute | solution.py:190
  43.0 0.9 %collective-permute-done.13.refs_5_ = bf16[128,512]{1,0:T(8,128)(2,1)S(1)} collective-permute-done((bf16[128,512]{1,0:T(8,128)(2,1)S(1)}, bf16[128,512]{1,0:T(8,128)(2,1)S(1)}, u32[]{:S(2)}, u32[]{:S(2)}) %collective-permute-start.13) | collective-permute-done | bytes 131104 | tf_op jit(solution)/shard_map/ppermute | solution.py:190
  43.9 0.0 collective-permute-done.14.refs_6_
  43.9 0.1 collective-permute-done.15.refs_7_
  44.1 0.1 sums.1
  44.2 0.1 collective-permute-start.16
  44.3 1.3 %collective-permute-done.16.refs_1_ = bf16[128,512]{1,0:T(8,128)(2,1)S(1)} collective-permute-done((bf16[128,512]{1,0:T(8,128)(2,1)S(1)}, bf16[128,512]{1,0:T(8,128)(2,1)S(1)}, u32[]{:S(2)}, u32[]{:S(2)}) %collective-permute-start.16) | collective-permute-done | bytes 131104 | tf_op jit(solution)/shard_map/ppermute | solution.py:190
  45.6 1.0 %finish.1 = bf16[256,512]{1,0:T(8,128)(2,1)} custom-call(bf16[256,256]{1,0:T(8,128)(2,1)S(1)} %get-tuple-element.30.place_ref, bf16[128,512]{1,0:T(8,128)(2,1)S(1)} %get-tuple-element.53.refs_0_, bf16[128,512]{1,0:T(8,128)(2,1)S(1)} %collective-permute-done.16.refs_1_), custom_call_target="tpu_custom_call" | custom-call | tf_op jit(solution)/shard_map/finish/pallas_call | solution.py:307
Async XLA Ops:
  0.0 13.2 %copy-start = (bf16[2048,2048]{1,0:T(8,128)(2,1)S(1)}, bf16[2048,2048]{1,0:T(8,128)(2,1)}, u32[]{:S(2)}) copy-start(bf16[2048,2048]{1,0:T(8,128)(2,1)} %refs_2_.6) | copy-start | bytes 25165828
  0.9 1.3 %copy-start.3 = (bf16[256,2048]{1,0:T(8,128)(2,1)S(1)}, bf16[256,2048]{1,0:T(8,128)(2,1)}, u32[]{:S(2)}) copy-start(bf16[256,2048]{1,0:T(8,128)(2,1)} %tokens_ref.1) | copy-start | bytes 3145732
  3.3 3.1 %collective-permute-start = (bf16[64,2176]{1,0:T(8,128)(2,1)S(1)}, bf16[64,2176]{1,0:T(8,128)(2,1)S(1)}, u32[]{:S(2)}, u32[]{:S(2)}) collective-permute-start(bf16[64,2176]{1,0:T(8,128)(2,1)S(1)} %get-tuple-element.32), channel_id=1, source_target_pairs={{0,4},{1,5},{2,6},{3,7},{4,0},{5,1},{6,2},{7,3},{8,12},{9,13},{10,... | collective-permute-start | bytes 835592 | tf_op jit(solution)/shard_map/ppermute | solution.py:190
  3.8 16.4 %collective-permute-start.7 = (bf16[64,2176]{1,0:T(8,128)(2,1)S(1)}, bf16[64,2176]{1,0:T(8,128)(2,1)S(1)}, u32[]{:S(2)}, u32[]{:S(2)}) collective-permute-start(bf16[64,2176]{1,0:T(8,128)(2,1)S(1)} %get-tuple-element.42), channel_id=1, source_target_pairs={{0,8},{1,9},{2,10},{3,11},{4,12},{5,13},{6,14},{7,15},{8,0},{9,1},... | collective-permute-start | bytes 835592 | tf_op jit(solution)/shard_map/ppermute | solution.py:190
  6.4 13.8 %collective-permute-start.8 = (bf16[64,2176]{1,0:T(8,128)(2,1)S(1)}, bf16[64,2176]{1,0:T(8,128)(2,1)S(1)}, u32[]{:S(2)}, u32[]{:S(2)}) collective-permute-start(bf16[64,2176]{1,0:T(8,128)(2,1)S(1)} %get-tuple-element.43), channel_id=1, source_target_pairs={{0,12},{1,13},{2,14},{3,15},{4,8},{5,9},{6,10},{7,11},{8,4},{9,5},... | collective-permute-start | bytes 835592 | tf_op jit(solution)/shard_map/ppermute | solution.py:190
  6.5 10.7 %copy-start.2 = (bf16[16,16,2048]{2,1,0:T(8,128)(2,1)S(1)}, bf16[16,16,2048]{2,1,0:T(8,128)(2,1)}, u32[]{:S(2)}) copy-start(bf16[16,16,2048]{2,1,0:T(8,128)(2,1)} %param.9) | copy-start | bytes 3145732
  8.7 11.5 %copy-start.1 = (bf16[16,2048,128]{2,1,0:T(8,128)(2,1)S(1)}, bf16[16,2048,128]{2,1,0:T(8,128)(2,1)}, u32[]{:S(2)}) copy-start(bf16[16,2048,128]{2,1,0:T(8,128)(2,1)} %refs_2_.7) | copy-start | bytes 25165828
  8.7 5.8 %collective-permute-start.1 = (f32[32,128]{1,0:T(8,128)S(1)}, f32[32,128]{1,0:T(8,128)S(1)}, u32[]{:S(2)}, u32[]{:S(2)}) collective-permute-start(f32[32,128]{1,0:T(8,128)S(1)} %get-tuple-element.35), channel_id=1, source_target_pairs={{0,2},{1,3},{2,0},{3,1},{4,6},{5,7},{6,4},{7,5},{8,10},{9,11},{10,... | collective-permute-start | bytes 49160 | tf_op jit(solution)/shard_map/ppermute | solution.py:190
  11.6 5.5 %collective-permute-start.2 = (f32[32,128]{1,0:T(8,128)S(1)}, f32[32,128]{1,0:T(8,128)S(1)}, u32[]{:S(2)}, u32[]{:S(2)}) collective-permute-start(f32[32,128]{1,0:T(8,128)S(1)} %get-tuple-element.36), channel_id=1, source_target_pairs={{0,3},{1,2},{2,1},{3,0},{4,7},{5,6},{6,5},{7,4},{8,11},{9,10},{10,... | collective-permute-start | bytes 49160 | tf_op jit(solution)/shard_map/ppermute | solution.py:190
  13.0 4.2 %collective-permute-start.3 = (f32[32,128]{1,0:T(8,128)S(1)}, f32[32,128]{1,0:T(8,128)S(1)}, u32[]{:S(2)}, u32[]{:S(2)}) collective-permute-start(f32[32,128]{1,0:T(8,128)S(1)} %get-tuple-element.37), channel_id=1, source_target_pairs={{0,1},{1,0},{2,3},{3,2},{4,5},{5,4},{6,7},{7,6},{8,9},{9,8},{10,11... | collective-permute-start | bytes 49160 | tf_op jit(solution)/shard_map/ppermute | solution.py:190
  17.5 14.5 %collective-permute-start.5 = (bf16[128,512]{1,0:T(8,128)(2,1)S(1)}, bf16[128,512]{1,0:T(8,128)(2,1)S(1)}, u32[]{:S(2)}, u32[]{:S(2)}) collective-permute-start(bf16[128,512]{1,0:T(8,128)(2,1)S(1)} %get-tuple-element.39), channel_id=1, source_target_pairs={{0,2},{1,3},{2,0},{3,1},{4,6},{5,7},{6,4},{7,5},{8,10},{9,11},{10,... | collective-permute-start | bytes 393224 | tf_op jit(solution)/shard_map/ppermute | solution.py:190
  18.9 15.0 %collective-permute-start.6 = (bf16[128,512]{1,0:T(8,128)(2,1)S(1)}, bf16[128,512]{1,0:T(8,128)(2,1)S(1)}, u32[]{:S(2)}, u32[]{:S(2)}) collective-permute-start(bf16[128,512]{1,0:T(8,128)(2,1)S(1)} %get-tuple-element.40), channel_id=1, source_target_pairs={{0,1},{1,0},{2,3},{3,2},{4,5},{5,4},{6,7},{7,6},{8,9},{9,8},{10,11... | collective-permute-start | bytes 393224 | tf_op jit(solution)/shard_map/ppermute | solution.py:190
  21.0 5.7 %collective-permute-start.9 = (f32[32,128]{1,0:T(8,128)S(1)}, f32[32,128]{1,0:T(8,128)S(1)}, u32[]{:S(2)}, u32[]{:S(2)}) collective-permute-start(f32[32,128]{1,0:T(8,128)S(1)} %get-tuple-element.46), channel_id=1, source_target_pairs={{0,1},{1,0},{2,3},{3,2},{4,5},{5,4},{6,7},{7,6},{8,9},{9,8},{10,11... | collective-permute-start | bytes 49160 | tf_op jit(solution)/shard_map/ppermute | solution.py:190
  21.8 7.8 %collective-permute-start.10 = (f32[32,128]{1,0:T(8,128)S(1)}, f32[32,128]{1,0:T(8,128)S(1)}, u32[]{:S(2)}, u32[]{:S(2)}) collective-permute-start(f32[32,128]{1,0:T(8,128)S(1)} %get-tuple-element.47), channel_id=1, source_target_pairs={{0,2},{1,3},{2,0},{3,1},{4,6},{5,7},{6,4},{7,5},{8,10},{9,11},{10,... | collective-permute-start | bytes 49160 | tf_op jit(solution)/shard_map/ppermute | solution.py:190
  24.4 5.7 %collective-permute-start.11 = (f32[32,128]{1,0:T(8,128)S(1)}, f32[32,128]{1,0:T(8,128)S(1)}, u32[]{:S(2)}, u32[]{:S(2)}) collective-permute-start(f32[32,128]{1,0:T(8,128)S(1)} %get-tuple-element.48), channel_id=1, source_target_pairs={{0,3},{1,2},{2,1},{3,0},{4,7},{5,6},{6,5},{7,4},{8,11},{9,10},{10,... | collective-permute-start | bytes 49160 | tf_op jit(solution)/shard_map/ppermute | solution.py:190
  26.7 9.7 %collective-permute-start.4 = (bf16[128,512]{1,0:T(8,128)(2,1)S(1)}, bf16[128,512]{1,0:T(8,128)(2,1)S(1)}, u32[]{:S(2)}, u32[]{:S(2)}) collective-permute-start(bf16[128,512]{1,0:T(8,128)(2,1)S(1)} %get-tuple-element.38.refs_3_), channel_id=1, source_target_pairs={{0,3},{1,2},{2,1},{3,0},{4,7},{5,6},{6,5},{7,4},{8,11},{9,10},{10,... | collective-permute-start | bytes 393224 | tf_op jit(solution)/shard_map/ppermute | solution.py:190
  30.5 12.5 %collective-permute-start.12 = (bf16[128,512]{1,0:T(8,128)(2,1)S(1)}, bf16[128,512]{1,0:T(8,128)(2,1)S(1)}, u32[]{:S(2)}, u32[]{:S(2)}) collective-permute-start(bf16[128,512]{1,0:T(8,128)(2,1)S(1)} %get-tuple-element.49), channel_id=1, source_target_pairs={{0,8},{1,9},{2,10},{3,11},{4,12},{5,13},{6,14},{7,15},{8,0},{9,1},... | collective-permute-start | bytes 393224 | tf_op jit(solution)/shard_map/ppermute | solution.py:190
  32.1 11.9 %collective-permute-start.13 = (bf16[128,512]{1,0:T(8,128)(2,1)S(1)}, bf16[128,512]{1,0:T(8,128)(2,1)S(1)}, u32[]{:S(2)}, u32[]{:S(2)}) collective-permute-start(bf16[128,512]{1,0:T(8,128)(2,1)S(1)} %get-tuple-element.50), channel_id=1, source_target_pairs={{0,10},{1,11},{2,8},{3,9},{4,14},{5,15},{6,12},{7,13},{8,2},{9,3},... | collective-permute-start | bytes 393224 | tf_op jit(solution)/shard_map/ppermute | solution.py:190
  32.1 11.8 %collective-permute-start.14 = (bf16[128,512]{1,0:T(8,128)(2,1)S(1)}, bf16[128,512]{1,0:T(8,128)(2,1)S(1)}, u32[]{:S(2)}, u32[]{:S(2)}) collective-permute-start(bf16[128,512]{1,0:T(8,128)(2,1)S(1)} %get-tuple-element.51), channel_id=1, source_target_pairs={{0,11},{1,10},{2,9},{3,8},{4,15},{5,14},{6,13},{7,12},{8,3},{9,2},... | collective-permute-start | bytes 393224 | tf_op jit(solution)/shard_map/ppermute | solution.py:190
  33.8 10.3 %collective-permute-start.15 = (bf16[128,512]{1,0:T(8,128)(2,1)S(1)}, bf16[128,512]{1,0:T(8,128)(2,1)S(1)}, u32[]{:S(2)}, u32[]{:S(2)}) collective-permute-start(bf16[128,512]{1,0:T(8,128)(2,1)S(1)} %get-tuple-element.52), channel_id=1, source_target_pairs={{0,9},{1,8},{2,11},{3,10},{4,13},{5,12},{6,15},{7,14},{8,1},{9,0},... | collective-permute-start | bytes 393224 | tf_op jit(solution)/shard_map/ppermute | solution.py:190
  44.2 1.4 %collective-permute-start.16 = (bf16[128,512]{1,0:T(8,128)(2,1)S(1)}, bf16[128,512]{1,0:T(8,128)(2,1)S(1)}, u32[]{:S(2)}, u32[]{:S(2)}) collective-permute-start(bf16[128,512]{1,0:T(8,128)(2,1)S(1)} %get-tuple-element.54), channel_id=1, source_target_pairs={{0,4},{1,5},{2,6},{3,7},{4,0},{5,1},{6,2},{7,3},{8,12},{9,13},{10,... | collective-permute-start | bytes 393224 | tf_op jit(solution)/shard_map/ppermute | solution.py:190
